TPU v7x, 256 devices: a whole 4x4x8 slice. The times are simulated.
256 devices in a mesh: tok: 16 (over y, z_lo), tp: 16 (over z_hi, x, core).
Axes of the slice: x: 4, y: 4, z: 8 (z_hi: 2, z_lo: 4; z = z_hi * 4 + z_lo), core: 2. Of those that a mesh axis runs over, the one named last changes fastest.
Arguments:
- hidden: bfloat16 [16384, 28672], P('tok', 'tp'), may hold values from -48 to 48, as said below
- signs: int32 [28672], P('tp'), may hold values from 0 to 1
Outputs:
- gram: float32 [28672, 128], P(('tok', 'tp'))
Inputs may be any that keep to these rules, and one draw needn't show every extreme that they name: `hidden`: Activations; finite.
All inputs are finite; a program needn't handle non-finite values.
Results may differ from a plain program's by a relative error of at most 0.0046.
Values may be sent and summed in bfloat16 or wider, within the bound.
No kernel may reach another device: no remote copies, remote signals or barrier semaphores. Data moves between devices by JAX's collectives and lax.ppermute only.
A program may use at most 64 MiB of HBM per device.

v0:
```python
import math

import jax
import jax.numpy as jnp
import numpy as np
from jax import lax
from jax.sharding import PartitionSpec as P

HAD_BIG = 1024
COLS = 128


def paley_table():
    modulus = 13
    residue_set = set((number * number % modulus for number in range(1, modulus)))
    character = np.array(
        [0.0] + [1.0 if number in residue_set else -1.0 for number in range(1, modulus)],
        dtype=np.float32,
    )
    offsets = (np.arange(modulus)[None, :] - np.arange(modulus)[:, None]) % modulus
    jacobsthal = character[offsets]
    top_row = np.concatenate(
        [np.zeros((1, 1), np.float32), np.ones((1, modulus), np.float32)], axis=1
    )
    lower_rows = np.concatenate([np.ones((modulus, 1), np.float32), jacobsthal], axis=1)
    conference = np.concatenate([top_row, lower_rows], axis=0)
    pair_one = np.array([[1.0, 1.0], [1.0, -1.0]], np.float32)
    pair_two = np.array([[1.0, -1.0], [-1.0, -1.0]], np.float32)
    table = np.kron(conference, pair_one) + np.kron(np.eye(modulus + 1, dtype=np.float32), pair_two)
    return table.astype(np.float32)


def sylvester_table(order):
    table = np.ones((1, 1), np.float32)
    basic = np.array([[1.0, 1.0], [1.0, -1.0]], np.float32)
    while table.shape[0] < order:
        table = np.kron(table, basic).astype(np.float32)
    return jnp.asarray(table, jnp.float32)


def rotate_rows(signed, small_table, big_table, factor):
    row_count = signed.shape[0]
    cube = signed.reshape(row_count, small_table.shape[0], big_table.shape[0])
    first = jnp.einsum("rab,cb->rac", cube, big_table, preferred_element_type=jnp.float32).astype(
        jnp.bfloat16
    )
    second = (
        jnp.einsum("rab,ca->rcb", first, small_table, preferred_element_type=jnp.float32) * factor
    )
    return second.astype(jnp.bfloat16).reshape(row_count, signed.shape[1])


def column_product(source, slab_rows, inverse):
    product = lax.dot_general(
        source, slab_rows, (((0,), (0,)), ((), ())), preferred_element_type=jnp.float32
    )
    return product * inverse


def body(hidden, signs):
    tp_count = lax.axis_size("tp")
    tok_count = lax.axis_size("tok")
    row_count = hidden.shape[0] // tp_count
    width_part = hidden.shape[1]
    total_width = width_part * tp_count
    sign_row = (1 - 2 * signs).astype(jnp.bfloat16)
    signed = hidden * sign_row[None, :]
    small_table = jnp.asarray(paley_table(), jnp.bfloat16)
    big_table = sylvester_table(HAD_BIG).astype(jnp.bfloat16)
    factor = 1.0 / math.sqrt(total_width)
    stacked = signed.reshape(tp_count, row_count, width_part)
    rotated = rotate_rows(
        lax.all_to_all(stacked, "tp", split_axis=0, concat_axis=2, tiled=True)[0],
        small_table,
        big_table,
        factor,
    )[None][0]
    inverse = 1.0 / (row_count * tp_count * tok_count)
    slab = rotated[:, :COLS]
    return lax.psum_scatter(
        column_product(rotated, slab, inverse), ("tok", "tp"), scatter_dimension=0, tiled=True
    )


def solution(mesh):
    placed = (P("tok", "tp"), P("tp"))
    return jax.shard_map(
        body, mesh=mesh, in_specs=placed, out_specs=P(("tok", "tp"), None), check_vma=False
    )
```

profile of v0, /device:TPU:1, one launch (start us, length us, event | category | flops | bytes accessed | tf_op | source)
XLA Modules:
  0.0 1490.9 jit_solution(12323990694476321982)
XLA Ops:
  6.5 0.0 reduce-scatter.2.cloned.1.call-start
  6.5 0.7 subtract_convert_fusion
  7.2 2.3 broadcast_multiply_fusion
  9.5 73.3 %all_to_all.15 = bf16[16,64,1792]{2,1,0:T(8,128)(2,1)S(1)} all-to-all(bf16[16,64,1792]{2,1,0:T(8,128)(2,1)S(1)} %bitcast.16), channel_id=1, replica_groups=mesh['tok'=16,'tp'=16] {'tp'}, dimensions={0} | all-to-all | bytes 7340032 | tf_op jit(solution)/shard_map/all_to_all | solution.py:73
  82.8 3.8 copy.6
  86.7 0.0 copy-start.1
  86.7 8.0 reshape_squeeze.3
  94.7 0.0 copy-done.1
  94.7 0.0 copy-start
  94.7 8.5 fusion.6
  103.2 0.0 copy-done
  103.2 3.0 multiply_convert_fusion
  106.2 2.3 copy.9
  108.5 6.4 convolution_multiply_fusion
  114.9 0.0 reduce-scatter.2.cloned.1.call-update
  114.9 1369.2 %reduce-scatter.2.cloned.1.call-done = f32[112,128]{1,0:T(8,128)} async-done(((f32[28672,128]{1,0:T(8,128)}), f32[112,128]{1,0:T(8,128)}) %reduce-scatter.2.cloned.1.call-update) | async-done | bytes 57360 | tf_op jit(solution)/shard_map/reduce_scatter | solution.py:80
Async XLA Ops:
  6.5 1477.6 %reduce-scatter.2.cloned.1.call-start = ((), (), s32[]{:S(2)}) async-start(), calls=%async_computation.2 | async-start | bytes 14737408 | tf_op jit(solution)/shard_map/reduce_scatter | solution.py:80
  86.7 8.0 copy-start.1
  94.7 8.5 copy-start
Sparse Core Ops, SparseCore 0:
  115.0 1368.9 reduce-scatter.1
where the time goes:
time: 1510 us; the launch traced here: 1490 us
  waiting for transfers between devices  1370 us (91%)
  blocking collectives  73.3 us (5%)
  matrix products  17.9 us (1%)
    reduce_scatter x1, waiting for transfers between devices, body(): lax.psum_scatter(column_product(rotated, slab, inverse), ('tok', 'tp'), s...  1370 us
    all_to_all x1, blocking collectives, body(): lax.all_to_all(stacked, 'tp', split_axis=0, concat_axis=2, tiled=True)[0]  73.3 us
  transfers between devices with their start and end apart: 1, of which 1 were waited for; matrix products, arithmetic and copies ran while one was open for 0% of the time, Pallas kernels for 0%

commit v1 on v0

v1 whole, which is shorter than its diff:
```python
import functools

import jax
import jax.numpy as jnp
import numpy as np
from jax import lax
from jax.experimental import pallas as pl
from jax.experimental.pallas import tpu as pltpu
from jax.sharding import Mesh, PartitionSpec as P

FF = 28672
TOKENS = 16384
BIG = 1024
SMALL = 28
COLS = 128
BLK = 256
N_TP = 16
N_TOK = 16
N_XC = 8
WIDTH = FF // N_TP
N_Q = WIDTH // BLK
ROWS = FF // (N_TP * N_TOK)
TOK = TOKENS // N_TOK
HALF = TOK // 2
GROUP = COLS // N_TOK
LANE = 128

BF = jnp.bfloat16
F32 = jnp.float32


def paley_table():
    modulus = 13
    residues = {n * n % modulus for n in range(1, modulus)}
    character = np.array(
        [0.0] + [1.0 if n in residues else -1.0 for n in range(1, modulus)], np.float32
    )
    offsets = (np.arange(modulus)[None, :] - np.arange(modulus)[:, None]) % modulus
    lower = np.concatenate([np.ones((modulus, 1), np.float32), character[offsets]], axis=1)
    top = np.concatenate([np.zeros((1, 1), np.float32), np.ones((1, modulus), np.float32)], axis=1)
    conference = np.concatenate([top, lower], axis=0)
    one = np.array([[1.0, 1.0], [1.0, -1.0]], np.float32)
    two = np.array([[1.0, -1.0], [-1.0, -1.0]], np.float32)
    return np.kron(conference, one) + np.kron(np.eye(modulus + 1, dtype=np.float32), two)


def sylvester(order):
    table = np.ones((1, 1), np.float32)
    while table.shape[0] < order:
        table = np.kron(table, np.array([[1.0, 1.0], [1.0, -1.0]], np.float32))
    return table


def fold_table():
    return np.repeat(paley_table()[0], BIG).reshape(N_TP, 1, WIDTH)


def window_table():
    h = sylvester(BLK)
    out = np.zeros((N_XC, BLK, 2, LANE), np.float32)
    for pl_ in range(N_XC):
        for z in range(2):
            start = ROWS * (pl_ + N_XC * z)
            out[pl_, :, z, :] = h[:, (start + np.arange(LANE)) % BLK]
    return out.reshape(N_XC, BLK, 2 * LANE)


def mix_table():
    q_all = np.kron(paley_table(), sylvester(4))
    n_q = q_all.shape[0]
    out = np.zeros((N_TP, 2, 2, N_TOK, N_Q, N_XC), np.float32)
    for p in range(N_TP):
        zh, pl_ = divmod(p, N_XC)
        for z in range(2):
            first = ROWS * (pl_ + N_XC * z) // BLK
            for v in range(2):
                i = min(first + v, N_Q - 1)
                for j in range(N_Q):
                    for m in range(N_XC):
                        q = (zh * N_XC + m) * N_Q + j
                        out[p, z, v, :, j, m] = q_all[np.arange(N_TOK) * N_Q + i, q]
    assert n_q == N_TOK * N_Q
    return out


def mix_big_table():
    small = mix_table()
    eye = np.eye(GROUP, dtype=np.float32)
    big = np.einsum("pzvkjm,ab->pzvkajmb", small, eye)
    return big.reshape(N_TP, 2 * 2 * N_TOK * GROUP, N_Q * N_XC * GROUP)


def fold_kernel(ids, x_ref, s_ref, w_ref, send_ref, keep_ref):
    step = pl.program_id(0)
    coef = (1 - 2 * s_ref[...]).astype(F32) * w_ref[0]
    rows = x_ref.shape[0]
    total = jnp.zeros((rows, LANE), F32)
    for j in range(WIDTH // LANE):
        cols = slice(j * LANE, (j + 1) * LANE)
        total = total + x_ref[:, cols].astype(F32) * coef[:, cols]

    per = HALF // rows

    @pl.when(step < per)
    def _():
        send_ref[pl.ds(pl.multiple_of(step * rows, rows), rows), :] = total.astype(BF)

    @pl.when(step >= per)
    def _():
        keep_ref[pl.ds(pl.multiple_of((step - per) * rows, rows), rows), :] = total


def fold(ids, hidden, signs, weights):
    rows = 256
    per = HALF // rows

    def place(i, ids):
        core = ids[1]
        half = jnp.where(i < per, 1 - core, core)
        return (half * per + i % per, 0)

    return pl.pallas_call(
        fold_kernel,
        grid_spec=pltpu.PrefetchScalarGridSpec(
            num_scalar_prefetch=1,
            grid=(TOK // rows,),
            in_specs=[
                pl.BlockSpec((rows, WIDTH), place),
                pl.BlockSpec((1, WIDTH), lambda i, ids: (0, 0)),
                pl.BlockSpec((1, 1, WIDTH), lambda i, ids: (ids[0], 0, 0)),
            ],
            out_specs=[
                pl.BlockSpec((HALF, LANE), lambda i, ids: (0, 0)),
                pl.BlockSpec((HALF, LANE), lambda i, ids: (0, 0)),
            ],
        ),
        out_shape=[
            jax.ShapeDtypeStruct((HALF, LANE), BF),
            jax.ShapeDtypeStruct((HALF, LANE), F32),
        ],
        name="fold",
    )(ids, hidden, signs, weights)


def outer_kernel(ids, mine, mine_z, other, other_z, x_ref, out_ref):
    core = ids[1]
    dims = (((0,), (0,)), ((), ()))
    dot = functools.partial(lax.dot_general, dimension_numbers=dims, preferred_element_type=F32)
    x_mine = x_ref[pl.ds(pl.multiple_of(core * HALF, HALF), HALF), :]
    x_other = x_ref[pl.ds(pl.multiple_of((1 - core) * HALF, HALF), HALF), :]
    total = dot(mine[...], x_mine) + dot(mine_z[...], x_mine)
    total = total + dot(other[...], x_other) + dot(other_z[...], x_other)
    out_ref[...] = total.astype(BF)


def outer(ids, mine, mine_z, other, other_z, hidden):
    tile = 256
    whole = pl.BlockSpec((HALF, LANE), lambda i, ids: (0, 0))
    return pl.pallas_call(
        outer_kernel,
        grid_spec=pltpu.PrefetchScalarGridSpec(
            num_scalar_prefetch=1,
            grid=(WIDTH // tile,),
            in_specs=[whole] * 4 + [pl.BlockSpec((TOK, tile), lambda i, ids: (0, i))],
            out_specs=pl.BlockSpec((COLS, tile), lambda i, ids: (0, i)),
        ),
        out_shape=jax.ShapeDtypeStruct((COLS, WIDTH), BF),
        name="outer",
    )(ids, mine, mine_z, other, other_z, hidden)


def gather_kernel(x_ref, s_ref, out_ref):
    terms = x_ref[...].astype(F32).reshape(N_TOK, GROUP, WIDTH)
    total = jnp.sum(terms, axis=0) * (1 - 2 * s_ref[...]).astype(F32)
    out_ref[...] = jnp.concatenate([total] * N_XC, axis=0).astype(BF)


def gathered(x, signs):
    return pl.pallas_call(
        gather_kernel,
        out_shape=jax.ShapeDtypeStruct((N_XC * GROUP, WIDTH), BF),
        name="sum_tok",
    )(x, signs)


def split_dot(lhs, value):
    high = value.astype(BF)
    low = (value - high.astype(F32)).astype(BF)
    dot = functools.partial(jnp.dot, preferred_element_type=F32)
    return dot(lhs, high) + dot(lhs, low)


def rotate_kernel(ids, g_ref, win_ref, mix_ref, out_ref):
    window = win_ref[0]
    parts = []
    for j in range(N_Q):
        block = g_ref[:, j * BLK : (j + 1) * BLK]
        parts.append(jnp.dot(block, window, preferred_element_type=F32))
    spread = jnp.concatenate(parts, axis=0)
    lanes = lax.broadcasted_iota(jnp.int32, (N_TOK * GROUP, LANE), 1)
    halves = []
    for z in range(2):
        start = ROWS * (ids[0] % N_XC + N_XC * z)
        both = split_dot(
            mix_ref[0, z * 2 * LANE : (z + 1) * 2 * LANE, :], spread[:, z * LANE : (z + 1) * LANE]
        )
        wrapped = start % BLK + lanes >= BLK
        mixed = jnp.where(wrapped, both[LANE:], both[:LANE])
        halves.append(mixed.reshape(N_TOK, 1, GROUP, LANE))
    out_ref[...] = jnp.concatenate(halves, axis=1).reshape(2 * N_TOK * GROUP, LANE)


def rotate(ids, g, windows, mix):
    return pl.pallas_call(
        rotate_kernel,
        grid_spec=pltpu.PrefetchScalarGridSpec(
            num_scalar_prefetch=1,
            grid=(1,),
            in_specs=[
                pl.BlockSpec((N_XC * GROUP, WIDTH), lambda i, ids: (0, 0)),
                pl.BlockSpec((1, BLK, 2 * LANE), lambda i, ids: (ids[0] % N_XC, 0, 0)),
                pl.BlockSpec(
                    (1, 4 * N_TOK * GROUP, N_Q * N_XC * GROUP), lambda i, ids: (ids[0], 0, 0)
                ),
            ],
            out_specs=pl.BlockSpec((2 * N_TOK * GROUP, LANE), lambda i, ids: (0, 0)),
        ),
        out_shape=jax.ShapeDtypeStruct((2 * N_TOK * GROUP, LANE), F32),
        name="rotate",
    )(ids, g, windows, mix)


def finish_kernel(x_ref, h_ref, out_ref):
    terms = x_ref[...].reshape(N_TOK, 2, GROUP, LANE)
    total = (terms[:, 0] + terms[:, 1]).reshape(COLS, LANE) * (1.0 / (FF * TOKENS))
    dims = (((0,), (0,)), ((), ()))
    dot = functools.partial(lax.dot_general, dimension_numbers=dims, preferred_element_type=F32)
    high = total.astype(BF)
    rest = total - high.astype(F32)
    mid = rest.astype(BF)
    low = (rest - mid.astype(F32)).astype(BF)
    table = h_ref[...]
    result = dot(high, table) + (dot(mid, table) + dot(low, table))
    out_ref[...] = result[:ROWS]


def finish(x, table):
    return pl.pallas_call(
        finish_kernel,
        out_shape=jax.ShapeDtypeStruct((ROWS, COLS), F32),
        name="finish",
    )(x, table)


TOK_AXES = ("y", "zl")
TP_AXES = ("zh", "x", "core")


def body(hidden, signs):
    p = lax.axis_index(TP_AXES).astype(jnp.int32)
    core = lax.axis_index("core").astype(jnp.int32)
    ids = jnp.stack([p, core])
    signs = signs.reshape(1, WIDTH)
    send, keep = fold(ids, hidden, signs, jnp.asarray(fold_table(), F32))

    swap = [(0, 1), (1, 0)]
    near = [(i, i ^ 1) for i in range(4)]
    far = [(i, i ^ 2) for i in range(4)]
    total = keep + lax.ppermute(send, "core", swap).astype(F32)
    total = total + lax.ppermute(total.astype(BF), "x", near).astype(F32)
    total = total + lax.ppermute(total.astype(BF), "x", far).astype(F32)
    mine = total.astype(BF)
    mine_z = lax.ppermute(mine, "zh", swap)
    other = lax.ppermute(mine, "core", swap)
    other_z = lax.ppermute(mine_z, "core", swap)

    wide = outer(ids, mine, mine_z, other, other_z, hidden)
    wide = lax.all_to_all(wide, TOK_AXES, split_axis=0, concat_axis=0, tiled=True)
    g = gathered(wide, signs)
    g = lax.all_to_all(g, ("x", "core"), split_axis=0, concat_axis=0, tiled=True)
    turned = rotate(ids, g, jnp.asarray(window_table(), BF), jnp.asarray(mix_big_table(), BF))
    turned = lax.all_to_all(turned, ("y", "zl", "zh"), split_axis=0, concat_axis=0, tiled=True)
    return finish(turned, jnp.asarray(sylvester(COLS), BF))


def solution(mesh):
    fine = Mesh(mesh.devices.reshape(4, 4, 2, 4, 2), ("y", "zl", "zh", "x", "core"))
    return jax.shard_map(
        body,
        mesh=fine,
        in_specs=(P(TOK_AXES, TP_AXES), P(TP_AXES)),
        out_specs=P(TOK_AXES + TP_AXES, None),
        check_vma=False,
    )
```

time: 1510 us -> 102 us (0.07); the launches traced: 1490 us -> 101 us
  waiting for transfers between devices: 1370 us -> 11.2 us
  blocking collectives: 73.3 us -> 48.8 us
  Pallas kernels: 0 us -> 18.7 us
  matrix products: 17.9 us -> 0 us
  starting transfers between devices: 0.01 us -> 16.8 us
    reduce_scatter x1 -> x0, waiting for transfers between devices: 1370 us -> none  [body(): lax.psum_scatter(column_product(rotated, slab, inverse), ('tok', 'tp'), s...]
    all_to_all x1 -> x3, blocking collectives: 73.3 us -> 48.8 us  [the longest x1 21.2 us: body(): lax.all_to_all(wide, TOK_AXES, split_axis=0, concat_axis=0, tiled=True)]
    pallas_call x0 -> x5, Pallas kernels: none -> 18.7 us  [the longest x1 7.24 us: outer(): pl.pallas_call(outer_kernel, grid_spec=pltpu.PrefetchScalarGridSpec(num_s...]
    dot_general x3 -> x0, matrix products: 17.9 us -> none  [the longest x1 8.54 us: rotate_rows(): jnp.einsum('rab,cb->rac', cube, big_table, preferred_element_type=jnp.flo...]
    ppermute x0 -> x6, starting transfers between devices: none -> 16.8 us  [the longest x1 5.26 us: body(): mine_z = lax.ppermute(mine, 'zh', swap)]
  transfers between devices with their start and end apart: 1 -> 6, of which waited for: 1 -> 4; matrix products, arithmetic and copies ran while one was open for 0% -> 0% of each run, Pallas kernels for 0% -> 0%
where the time goes in v1:
time: 102 us; the launch traced here: 101 us
  blocking collectives  48.8 us (48%)
  Pallas kernels  18.7 us (18%)
  starting transfers between devices  16.8 us (16%)
  waiting for transfers between devices  11.2 us (11%)
  other arithmetic  3.62 us (4%)
  local copies, waits for them, and re-layouts  1.95 us (2%)
    all_to_all x1, blocking collectives, body(): lax.all_to_all(wide, TOK_AXES, split_axis=0, concat_axis=0, tiled=True)  21.2 us
    all_to_all x1, blocking collectives, body(): lax.all_to_all(turned, ('y', 'zl', 'zh'), split_axis=0, concat_axis=0, ti...  15.3 us
    all_to_all x1, blocking collectives, body(): lax.all_to_all(g, ('x', 'core'), split_axis=0, concat_axis=0, tiled=True)  12.3 us
    pallas_call x1, Pallas kernels, outer(): pl.pallas_call(outer_kernel, grid_spec=pltpu.PrefetchScalarGridSpec(num_s...  7.24 us
    ppermute x1, starting transfers between devices, body(): mine_z = lax.ppermute(mine, 'zh', swap)  5.26 us
    ppermute x1, waiting for transfers between devices, body(): total = total + lax.ppermute(total.astype(BF), 'x', near).astype(F32)  4.71 us
    pallas_call x1, Pallas kernels, fold(): pl.pallas_call(fold_kernel, grid_spec=pltpu.PrefetchScalarGridSpec(num_sc...  4.68 us
    ppermute x1, starting transfers between devices, body(): other_z = lax.ppermute(mine_z, 'core', swap)  4.46 us
  transfers between devices with their start and end apart: 6, of which 4 were waited for; matrix products, arithmetic and copies ran while one was open for 0% of the time, Pallas kernels for 0%

profile of v1, /device:TPU:1, one launch (start us, length us, event | category | flops | bytes accessed | tf_op | source)
XLA Modules:
  0.0 101.1 jit_solution(9389652264207857137)
XLA Ops:
  0.0 1.3 %reshape.9.s_ref = s32[1,1792]{1,0:T(1,128)} reshape(s32[1792]{0:T(1024)} %param.7) | data formatting | bytes 14336 | tf_op jit(solution)/shard_map/reshape | solution.py:263
  1.3 0.6 pad_add_fusion.ids
  1.9 4.7 %fold.1 = (bf16[512,128]{1,0:T(8,128)(2,1)}, f32[512,128]{1,0:T(8,128)}) custom-call(s32[2]{0:T(128)} %pad_add_fusion.ids, bf16[1024,1792]{1,0:T(8,128)(2,1)} %x_ref.3, s32[1,1792]{1,0:T(1,128)} %reshape.9.s_ref, f32[16,1,1792]{2,1,0:T(1,128)} %constant.23.clone.w_ref), custom_call_target="tpu_custom_call" | custom-call | tf_op jit(solution)/shard_map/fold/pallas_call | solution.py:122
  6.6 3.2 %collective-permute-start = (bf16[512,128]{1,0:T(8,128)(2,1)}, bf16[512,128]{1,0:T(8,128)(2,1)S(1)}, u32[]{:S(2)}, u32[]{:S(2)}) collective-permute-start(bf16[512,128]{1,0:T(8,128)(2,1)} %get-tuple-element.8), channel_id=1, source_target_pairs={{0,1},{1,0},{2,3},{3,2},{4,5},{5,4},{6,7},{7,6},{8,9},{9,8},{10,11... | collective-permute-start | bytes 393224 | tf_op jit(solution)/shard_map/ppermute | solution.py:269
  9.8 1.2 %collective-permute-done = bf16[512,128]{1,0:T(8,128)(2,1)S(1)} collective-permute-done((bf16[512,128]{1,0:T(8,128)(2,1)}, bf16[512,128]{1,0:T(8,128)(2,1)S(1)}, u32[]{:S(2)}, u32[]{:S(2)}) %collective-permute-start) | collective-permute-done | bytes 131104 | tf_op jit(solution)/shard_map/ppermute | solution.py:269
  11.0 1.0 fusion
  12.0 0.1 collective-permute-start.1
  12.1 4.7 %collective-permute-done.1 = bf16[512,128]{1,0:T(8,128)(2,1)S(1)} collective-permute-done((bf16[512,128]{1,0:T(8,128)(2,1)S(1)}, bf16[512,128]{1,0:T(8,128)(2,1)S(1)}, u32[]{:S(2)}, u32[]{:S(2)}) %collective-permute-start.1) | collective-permute-done | bytes 131104 | tf_op jit(solution)/shard_map/ppermute | solution.py:270
  16.8 1.0 fusion.1
  17.8 1.1 %collective-permute-start.2 = (bf16[512,128]{1,0:T(8,128)(2,1)S(1)}, bf16[512,128]{1,0:T(8,128)(2,1)S(1)}, u32[]{:S(2)}, u32[]{:S(2)}) collective-permute-start(bf16[512,128]{1,0:T(8,128)(2,1)S(1)} %fusion.1), channel_id=1, source_target_pairs={{0,4},{2,6},{4,0},{6,2},{1,5},{3,7},{5,1},{7,3},{8,12},{10,14},{12... | collective-permute-start | bytes 393224 | tf_op jit(solution)/shard_map/ppermute | solution.py:271
  18.9 4.3 %collective-permute-done.2 = bf16[512,128]{1,0:T(8,128)(2,1)S(1)} collective-permute-done((bf16[512,128]{1,0:T(8,128)(2,1)S(1)}, bf16[512,128]{1,0:T(8,128)(2,1)S(1)}, u32[]{:S(2)}, u32[]{:S(2)}) %collective-permute-start.2) | collective-permute-done | bytes 131104 | tf_op jit(solution)/shard_map/ppermute | solution.py:271
  23.2 1.0 %add_convert_fusion.mine = bf16[512,128]{1,0:T(8,128)(2,1)S(1)} fusion(bf16[512,128]{1,0:T(8,128)(2,1)S(1)} %collective-permute-done.2, bf16[512,128]{1,0:T(8,128)(2,1)S(1)} %collective-permute-done.1, f32[512,128]{1,0:T(8,128)} %get-tuple-element.7, bf16[512,128]{1,0:T(8,128)(2,1)S(1)} %collective-permute-done), kind=kLoop, calls=%fused_computation | loop fusion | flops 458752 | bytes 786432 | tf_op jit(solution)/shard_map/convert_element_type | solution.py:272
  24.3 0.0 copy-start
  24.3 5.3 %collective-permute-start.3 = (bf16[512,128]{1,0:T(8,128)(2,1)S(1)}, bf16[512,128]{1,0:T(8,128)(2,1)S(1)}, u32[]{:S(2)}, u32[]{:S(2)}) collective-permute-start(bf16[512,128]{1,0:T(8,128)(2,1)S(1)} %add_convert_fusion.mine), channel_id=1, source_target_pairs={{0,8},{8,0},{1,9},{9,1},{2,10},{10,2},{3,11},{11,3},{4,12},{12,4},... | collective-permute-start | bytes 393224 | tf_op jit(solution)/shard_map/ppermute | solution.py:273
  29.5 2.6 %collective-permute-start.4 = (bf16[512,128]{1,0:T(8,128)(2,1)S(1)}, bf16[512,128]{1,0:T(8,128)(2,1)S(1)}, u32[]{:S(2)}, u32[]{:S(2)}) collective-permute-start(bf16[512,128]{1,0:T(8,128)(2,1)S(1)} %add_convert_fusion.mine), channel_id=1, source_target_pairs={{0,1},{1,0},{2,3},{3,2},{4,5},{5,4},{6,7},{7,6},{8,9},{9,8},{10,11... | collective-permute-start | bytes 393224 | tf_op jit(solution)/shard_map/ppermute | solution.py:274
  32.2 0.0 collective-permute-done.3.mine_z
  32.2 0.0 copy-start.1
  32.2 4.5 %collective-permute-start.5 = (bf16[512,128]{1,0:T(8,128)(2,1)S(1)}, bf16[512,128]{1,0:T(8,128)(2,1)S(1)}, u32[]{:S(2)}, u32[]{:S(2)}) collective-permute-start(bf16[512,128]{1,0:T(8,128)(2,1)S(1)} %collective-permute-done.3.mine_z), channel_id=1, source_target_pairs={{0,1},{1,0},{2,3},{3,2},{4,5},{5,4},{6,7},{7,6},{8,9},{9,8},{10,11... | collective-permute-start | bytes 393224 | tf_op jit(solution)/shard_map/ppermute | solution.py:275
  36.6 0.0 collective-permute-done.4.other
  36.7 0.0 copy-start.2
  36.7 1.0 collective-permute-done.5.other_z
  37.6 0.0 copy-done
  37.6 0.0 copy-done.1
  37.6 0.0 copy-done.2
  37.6 0.0 copy-start.3
  37.6 0.6 copy-done.3
  38.3 7.2 %outer.1 = bf16[128,1792]{1,0:T(8,128)(2,1)} custom-call(s32[2]{0:T(128)} %pad_add_fusion.ids, bf16[512,128]{1,0:T(8,128)(2,1)} %copy-done, bf16[512,128]{1,0:T(8,128)(2,1)} %copy-done.1, bf16[512,128]{1,0:T(8,128)(2,1)} %copy-done.2, bf16[512,128]{1,0:T(8,128)(2,1)} %copy-done.3, bf16[1024,1792]{1,0:T(8,128)(2,1)} %x_ref.3), custom_call_target="tpu_custom_call" | custom-call | tf_op jit(solution)/shard_map/outer/pallas_call | solution.py:159
  45.5 21.2 %all_to_all.33 = bf16[16,8,1792]{2,1,0:T(8,128)(2,1)} all-to-all(bf16[16,8,1792]{2,1,0:T(8,128)(2,1)} %bitcast.8), channel_id=1, replica_groups=mesh['y'=4,'zl'=4,'zh'=2,'x'=4,'core'=2] {'y','zl'}, dimensions={0} | all-to-all | bytes 917504 | tf_op jit(solution)/shard_map/all_to_all | solution.py:278
  66.8 1.8 %sum_tok.1 = bf16[64,1792]{1,0:T(8,128)(2,1)} custom-call(bf16[128,1792]{1,0:T(8,128)(2,1)} %bitcast.9, s32[1,1792]{1,0:T(1,128)} %reshape.9.s_ref), custom_call_target="tpu_custom_call" | custom-call | tf_op jit(solution)/shard_map/sum_tok/pallas_call | solution.py:179
  68.5 12.3 %all_to_all.34 = bf16[8,8,1792]{2,1,0:T(8,128)(2,1)} all-to-all(bf16[8,8,1792]{2,1,0:T(8,128)(2,1)} %bitcast.11), channel_id=1, replica_groups=mesh['y'=4,'zl'=4,'zh'=2,'x'=4,'core'=2] {'x','core'}, dimensions={0} | all-to-all | bytes 458752 | tf_op jit(solution)/shard_map/all_to_all | solution.py:280
  80.8 3.2 %rotate.1 = f32[256,128]{1,0:T(8,128)} custom-call(s32[2]{0:T(128)} %pad_add_fusion.ids, bf16[64,1792]{1,0:T(8,128)(2,1)} %bitcast.10, bf16[8,256,256]{2,1,0:T(8,128)(2,1)} %constant.24.clone.win_ref, bf16[16,512,448]{2,1,0:T(8,128)(2,1)} %constant.25.clone.mix_ref), custom_call_target="tpu_custom_call" | custom-call | tf_op jit(solution)/shard_map/rotate/pallas_call | solution.py:214
  84.0 15.3 %all_to_all.35 = f32[32,8,128]{2,1,0:T(8,128)} all-to-all(f32[32,8,128]{2,1,0:T(8,128)} %bitcast.12), channel_id=1, replica_groups=mesh['y'=4,'zl'=4,'zh'=2,'x'=4,'core'=2] {'y','zl','zh'}, dimensions={0} | all-to-all | bytes 262144 | tf_op jit(solution)/shard_map/all_to_all | solution.py:282
  99.3 1.8 %finish.1 = f32[112,128]{1,0:T(8,128)} custom-call(f32[256,128]{1,0:T(8,128)} %bitcast.13, bf16[128,128]{1,0:T(8,128)(2,1)} %constant.26.clone.h_ref), custom_call_target="tpu_custom_call" | custom-call | tf_op jit(solution)/shard_map/finish/pallas_call | solution.py:248
Async XLA Ops:
  6.6 4.4 %collective-permute-start = (bf16[512,128]{1,0:T(8,128)(2,1)}, bf16[512,128]{1,0:T(8,128)(2,1)S(1)}, u32[]{:S(2)}, u32[]{:S(2)}) collective-permute-start(bf16[512,128]{1,0:T(8,128)(2,1)} %get-tuple-element.8), channel_id=1, source_target_pairs={{0,1},{1,0},{2,3},{3,2},{4,5},{5,4},{6,7},{7,6},{8,9},{9,8},{10,11... | collective-permute-start | bytes 393224 | tf_op jit(solution)/shard_map/ppermute | solution.py:269
  12.0 4.8 %collective-permute-start.1 = (bf16[512,128]{1,0:T(8,128)(2,1)S(1)}, bf16[512,128]{1,0:T(8,128)(2,1)S(1)}, u32[]{:S(2)}, u32[]{:S(2)}) collective-permute-start(bf16[512,128]{1,0:T(8,128)(2,1)S(1)} %fusion), channel_id=1, source_target_pairs={{0,2},{2,0},{4,6},{6,4},{1,3},{3,1},{5,7},{7,5},{8,10},{10,8},{12,... | collective-permute-start | bytes 393224 | tf_op jit(solution)/shard_map/ppermute | solution.py:270
  17.8 5.4 %collective-permute-start.2 = (bf16[512,128]{1,0:T(8,128)(2,1)S(1)}, bf16[512,128]{1,0:T(8,128)(2,1)S(1)}, u32[]{:S(2)}, u32[]{:S(2)}) collective-permute-start(bf16[512,128]{1,0:T(8,128)(2,1)S(1)} %fusion.1), channel_id=1, source_target_pairs={{0,4},{2,6},{4,0},{6,2},{1,5},{3,7},{5,1},{7,3},{8,12},{10,14},{12... | collective-permute-start | bytes 393224 | tf_op jit(solution)/shard_map/ppermute | solution.py:271
  24.3 13.4 %copy-start = (bf16[512,128]{1,0:T(8,128)(2,1)}, bf16[512,128]{1,0:T(8,128)(2,1)S(1)}, u32[]{:S(2)}) copy-start(bf16[512,128]{1,0:T(8,128)(2,1)S(1)} %add_convert_fusion.mine) | copy-start | bytes 393220
  24.3 7.9 %collective-permute-start.3 = (bf16[512,128]{1,0:T(8,128)(2,1)S(1)}, bf16[512,128]{1,0:T(8,128)(2,1)S(1)}, u32[]{:S(2)}, u32[]{:S(2)}) collective-permute-start(bf16[512,128]{1,0:T(8,128)(2,1)S(1)} %add_convert_fusion.mine), channel_id=1, source_target_pairs={{0,8},{8,0},{1,9},{9,1},{2,10},{10,2},{3,11},{11,3},{4,12},{12,4},... | collective-permute-start | bytes 393224 | tf_op jit(solution)/shard_map/ppermute | solution.py:273
  29.5 7.1 %collective-permute-start.4 = (bf16[512,128]{1,0:T(8,128)(2,1)S(1)}, bf16[512,128]{1,0:T(8,128)(2,1)S(1)}, u32[]{:S(2)}, u32[]{:S(2)}) collective-permute-start(bf16[512,128]{1,0:T(8,128)(2,1)S(1)} %add_convert_fusion.mine), channel_id=1, source_target_pairs={{0,1},{1,0},{2,3},{3,2},{4,5},{5,4},{6,7},{7,6},{8,9},{9,8},{10,11... | collective-permute-start | bytes 393224 | tf_op jit(solution)/shard_map/ppermute | solution.py:274
  32.2 5.5 %copy-start.1 = (bf16[512,128]{1,0:T(8,128)(2,1)}, bf16[512,128]{1,0:T(8,128)(2,1)S(1)}, u32[]{:S(2)}) copy-start(bf16[512,128]{1,0:T(8,128)(2,1)S(1)} %collective-permute-done.3.mine_z) | copy-start | bytes 393220
  32.2 5.4 %collective-permute-start.5 = (bf16[512,128]{1,0:T(8,128)(2,1)S(1)}, bf16[512,128]{1,0:T(8,128)(2,1)S(1)}, u32[]{:S(2)}, u32[]{:S(2)}) collective-permute-start(bf16[512,128]{1,0:T(8,128)(2,1)S(1)} %collective-permute-done.3.mine_z), channel_id=1, source_target_pairs={{0,1},{1,0},{2,3},{3,2},{4,5},{5,4},{6,7},{7,6},{8,9},{9,8},{10,11... | collective-permute-start | bytes 393224 | tf_op jit(solution)/shard_map/ppermute | solution.py:275
  36.7 1.0 copy-start.2
  37.6 0.6 copy-start.3

commit v2 on v1

v2 whole, which is shorter than its diff:
```python
import functools

import jax
import jax.numpy as jnp
import numpy as np
from jax import lax
from jax.experimental import pallas as pl
from jax.experimental.pallas import tpu as pltpu
from jax.sharding import Mesh, PartitionSpec as P

FF = 28672
TOKENS = 16384
BIG = 1024
SMALL = 28
COLS = 128
BLK = 256
N_TP = 16
N_TOK = 16
N_XC = 8
RING = 4
WIDTH = FF // N_TP
N_Q = WIDTH // BLK
ROWS = FF // (N_TP * N_TOK)
TOK = TOKENS // N_TOK
HALF = TOK // 2
GROUP = COLS // N_TOK
LANE = 128
N_L = WIDTH // LANE
FOLDED = WIDTH // 2

BF = jnp.bfloat16
F32 = jnp.float32
TOK_AXES = ("y", "zl")
TP_AXES = ("zh", "x", "core")
VMEM = pl.BlockSpec(memory_space=pltpu.VMEM)
HBM = pl.BlockSpec(memory_space=pltpu.HBM)
LITTLE = pltpu.CompilerParams(vmem_limit_bytes=8 << 20)


def paley_table():
    modulus = 13
    residues = {n * n % modulus for n in range(1, modulus)}
    character = np.array(
        [0.0] + [1.0 if n in residues else -1.0 for n in range(1, modulus)], np.float32
    )
    offsets = (np.arange(modulus)[None, :] - np.arange(modulus)[:, None]) % modulus
    lower = np.concatenate([np.ones((modulus, 1), np.float32), character[offsets]], axis=1)
    top = np.concatenate([np.zeros((1, 1), np.float32), np.ones((1, modulus), np.float32)], axis=1)
    conference = np.concatenate([top, lower], axis=0)
    one = np.array([[1.0, 1.0], [1.0, -1.0]], np.float32)
    two = np.array([[1.0, -1.0], [-1.0, -1.0]], np.float32)
    return np.kron(conference, one) + np.kron(np.eye(modulus + 1, dtype=np.float32), two)


def sylvester(order):
    table = np.ones((1, 1), np.float32)
    while table.shape[0] < order:
        table = np.kron(table, np.array([[1.0, 1.0], [1.0, -1.0]], np.float32))
    return table


def window_table():
    h = sylvester(BLK)
    out = np.zeros((N_XC, BLK, 2, LANE), np.float32)
    for member in range(N_XC):
        for z in range(2):
            start = ROWS * (member + N_XC * z)
            out[member, :, z, :] = h[:, (start + np.arange(LANE)) % BLK]
    return out.reshape(N_XC, BLK, 2 * LANE)


def mix_table():
    q_all = np.kron(paley_table(), sylvester(BIG // BLK))
    small = np.zeros((N_TP, 2, 2, N_TOK, N_Q, N_XC), np.float32)
    for p in range(N_TP):
        zh, member = divmod(p, N_XC)
        x, core = divmod(member, 2)
        for z in range(2):
            first = ROWS * (member + N_XC * z) // BLK
            for v in range(2):
                i = min(first + v, N_Q - 1)
                for j in range(N_Q):
                    for slot in range(N_XC):
                        s, e = divmod(slot, 2)
                        source = ((x - s) % RING) * 2 + (core ^ e)
                        q = (zh * N_XC + source) * N_Q + j
                        small[p, z, v, :, j, slot] = q_all[np.arange(N_TOK) * N_Q + i, q]
    eye = np.eye(GROUP, dtype=np.float32)
    big = np.einsum("pzvkjm,ab->pzvkajmb", small, eye)
    return big.reshape(N_TP, 4 * LANE, N_Q * N_XC * GROUP)


def in_hbm(x):
    return pltpu.with_memory_space_constraint(x, pltpu.HBM)


def fold_kernel(x_ref, s_ref, send_ref, keep_ref, held_ref, sign_ref, raw, sems, sign_sem):
    core = lax.axis_index("core")
    p = lax.axis_index("zh") * N_XC + lax.axis_index("x") * 2 + core
    sign_copy = pltpu.make_async_copy(s_ref, raw, sign_sem)
    sign_copy.start()
    rows = FOLD_ROWS
    count = TOK // rows
    per = count // 2
    copies, starts = [], []
    for i in range(count):
        half = 1 - core if i < per else core
        start = pl.multiple_of(half * HALF + (i % per) * rows, rows)
        here = pl.ds(start, rows)
        copy = pltpu.make_async_copy(x_ref.at[here, :], held_ref.at[here, :], sems.at[i])
        copy.start()
        copies.append(copy)
        starts.append(here)
    sign_copy.wait()
    first_row = paley_table()[0]
    coefs = []
    for j in range(N_L):
        block = (p * N_L + j) // (BIG // LANE)
        weight = jnp.float32(1.0)
        for a in range(SMALL):
            if first_row[a] != 1.0:
                weight = jnp.where(block == a, jnp.float32(first_row[a]), weight)
        sign = (1 - 2 * raw[j : j + 1, :]).astype(F32)
        sign_ref[j : j + 1, :] = sign
        coefs.append(sign * weight)
    for i in range(count):
        copies[i].wait()
        total = jnp.zeros((rows, LANE), F32)
        for j in range(N_L):
            total = total + held_ref[starts[i], j * LANE : (j + 1) * LANE].astype(F32) * coefs[j]
        place = slice((i % per) * rows, (i % per + 1) * rows)
        if i < per:
            send_ref[place, :] = total.astype(BF)
        else:
            keep_ref[place, :] = total


FOLD_ROWS = 128


def fold(hidden, signs):
    count = TOK // FOLD_ROWS
    return pl.pallas_call(
        fold_kernel,
        in_specs=[HBM, HBM],
        out_specs=[VMEM] * 4,
        out_shape=[
            jax.ShapeDtypeStruct((HALF, LANE), BF),
            jax.ShapeDtypeStruct((HALF, LANE), F32),
            jax.ShapeDtypeStruct((TOK, WIDTH), BF),
            jax.ShapeDtypeStruct((N_L, LANE), F32),
        ],
        scratch_shapes=[
            pltpu.VMEM((N_L, LANE), jnp.int32),
            pltpu.SemaphoreType.DMA((count,)),
            pltpu.SemaphoreType.DMA,
        ],
        compiler_params=LITTLE,
        cost_estimate=pl.CostEstimate(
            flops=2 * TOK * WIDTH, bytes_accessed=2 * TOK * WIDTH, transcendentals=0
        ),
        name="fold",
    )(in_hbm(hidden), in_hbm(signs))


def sum_core_kernel(own, a, out_ref, short_ref):
    total = own[...] + a[...].astype(F32)
    out_ref[...] = total
    short_ref[...] = total.astype(BF)


def sum_core(own, term):
    return pl.pallas_call(
        sum_core_kernel,
        in_specs=[VMEM] * 2,
        out_specs=[VMEM] * 2,
        out_shape=[
            jax.ShapeDtypeStruct((HALF, LANE), F32),
            jax.ShapeDtypeStruct((HALF, LANE), BF),
        ],
        compiler_params=LITTLE,
        name="sum_core",
    )(own, term)


def sum_x_kernel(own, a, b, c, out_ref):
    total = (own[...] + a[...].astype(F32)) + (b[...].astype(F32) + c[...].astype(F32))
    out_ref[...] = total.T.astype(BF)


def sum_x(own, terms):
    return pl.pallas_call(
        sum_x_kernel,
        in_specs=[VMEM] * 4,
        out_specs=VMEM,
        out_shape=jax.ShapeDtypeStruct((LANE, HALF), BF),
        compiler_params=LITTLE,
        name="sum_x",
    )(own, *terms)


def tiles(ref):
    for i in range(N_Q):
        yield slice(i * BLK, (i + 1) * BLK), ref[:, i * BLK : (i + 1) * BLK]


def outer_kernel(mine, other, x_ref, out_ref):
    core = lax.axis_index("core")
    mine, other = mine[...], other[...]
    left = jnp.concatenate(
        [jnp.where(core == 0, mine, other), jnp.where(core == 0, other, mine)], axis=1
    )
    for cols, block in tiles(x_ref):
        out_ref[:, cols] = jnp.dot(left, block, preferred_element_type=F32)


def cost(tokens):
    return pl.CostEstimate(
        flops=2 * COLS * tokens * WIDTH, bytes_accessed=2 * tokens * WIDTH, transcendentals=0
    )


def outer(mine, other, hidden):
    return pl.pallas_call(
        outer_kernel,
        in_specs=[VMEM] * 3,
        out_specs=VMEM,
        out_shape=jax.ShapeDtypeStruct((COLS, WIDTH), F32),
        compiler_params=LITTLE,
        cost_estimate=cost(TOK),
        name="outer",
    )(mine, other, hidden)


def half_of(x_ref, half):
    return x_ref.at[pl.ds(pl.multiple_of(half * HALF, HALF), HALF), :]


def outer_mine_kernel(mine, acc_ref, x_ref, out_ref):
    left = mine[...]
    for cols, block in tiles(half_of(x_ref, lax.axis_index("core"))):
        out_ref[:, cols] = acc_ref[:, cols] + jnp.dot(left, block, preferred_element_type=F32)


def outer_mine(mine, acc, hidden):
    return pl.pallas_call(
        outer_mine_kernel,
        in_specs=[VMEM] * 3,
        out_specs=VMEM,
        out_shape=jax.ShapeDtypeStruct((COLS, WIDTH), F32),
        compiler_params=LITTLE,
        cost_estimate=cost(HALF),
        name="outer_mine",
    )(mine, acc, hidden)


def outer_other_kernel(other, acc_ref, x_ref, own_ref, s1_ref, s2_ref, s3_ref, total):
    left = other[...]
    y = lax.axis_index("y")
    per = COLS // RING
    for cols, block in tiles(half_of(x_ref, 1 - lax.axis_index("core"))):
        total[:, cols] = acc_ref[:, cols] + jnp.dot(left, block, preferred_element_type=F32)
    for s, ref in enumerate((own_ref, s1_ref, s2_ref, s3_ref)):
        start = pl.multiple_of((y + s) % RING * per, per)
        ref[...] = total[pl.ds(start, per), :].astype(ref.dtype)


def outer_other(other, acc, hidden):
    per = COLS // RING
    return pl.pallas_call(
        outer_other_kernel,
        in_specs=[VMEM] * 3,
        out_specs=[VMEM] * RING,
        out_shape=[jax.ShapeDtypeStruct((per, WIDTH), F32)]
        + [jax.ShapeDtypeStruct((per, WIDTH), BF)] * (RING - 1),
        scratch_shapes=[pltpu.VMEM((COLS, WIDTH), F32)],
        compiler_params=LITTLE,
        cost_estimate=cost(HALF),
        name="outer_other",
    )(other, acc, hidden)


def pack(x):
    return jnp.concatenate([x[:, :FOLDED], x[:, FOLDED:]], axis=0)


def unpack(x):
    x = x.astype(F32)
    return jnp.concatenate([x[:GROUP], x[GROUP:]], axis=1)


def sum_y_kernel(own, a, b, c, own_ref, s1_ref, s2_ref, s3_ref, total):
    total[...] = (own[...] + a[...].astype(F32)) + (b[...].astype(F32) + c[...].astype(F32))
    zl = lax.axis_index("zl")
    for s, ref in enumerate((own_ref, s1_ref, s2_ref, s3_ref)):
        start = pl.multiple_of((zl + s) % RING * GROUP, GROUP)
        part = total[pl.ds(start, GROUP), :]
        if s == 0:
            ref[...] = part
        else:
            ref[...] = pack(part).astype(BF)


def sum_y(own, terms):
    return pl.pallas_call(
        sum_y_kernel,
        in_specs=[VMEM] * RING,
        out_specs=[VMEM] * RING,
        out_shape=[jax.ShapeDtypeStruct((GROUP, WIDTH), F32)]
        + [jax.ShapeDtypeStruct((2 * GROUP, FOLDED), BF)] * (RING - 1),
        scratch_shapes=[pltpu.VMEM((COLS // RING, WIDTH), F32)],
        compiler_params=LITTLE,
        name="sum_y",
    )(own, *terms)


def sum_z_kernel(own, a, b, c, s_ref, out_ref):
    total = (own[...] + unpack(a[...])) + (unpack(b[...]) + unpack(c[...]))
    sign = jnp.concatenate([s_ref[j : j + 1, :] for j in range(N_L)], axis=1)
    out_ref[...] = pack(total * sign).astype(BF)


def sum_z(own, terms, signs):
    return pl.pallas_call(
        sum_z_kernel,
        in_specs=[VMEM] * (RING + 1),
        out_specs=VMEM,
        out_shape=jax.ShapeDtypeStruct((2 * GROUP, FOLDED), BF),
        compiler_params=LITTLE,
        name="sum_z",
    )(own, *terms, signs)


def split_dot(lhs, value):
    high = value.astype(BF)
    low = (value - high.astype(F32)).astype(BF)
    dot = functools.partial(jnp.dot, preferred_element_type=F32)
    return dot(lhs, high) + dot(lhs, low)


def tables_kernel(win_hbm, mix_hbm, win_ref, mix_ref, sems):
    member = lax.axis_index("x") * 2 + lax.axis_index("core")
    p = lax.axis_index("zh") * N_XC + member
    copies = [
        pltpu.make_async_copy(win_hbm.at[member], win_ref, sems.at[0]),
        pltpu.make_async_copy(mix_hbm.at[p], mix_ref, sems.at[1]),
    ]
    for copy in copies:
        copy.start()
    for copy in copies:
        copy.wait()


def tables():
    return pl.pallas_call(
        tables_kernel,
        in_specs=[HBM, HBM],
        out_specs=[VMEM, VMEM],
        out_shape=[
            jax.ShapeDtypeStruct((BLK, 2 * LANE), BF),
            jax.ShapeDtypeStruct((4 * LANE, N_Q * N_XC * GROUP), BF),
        ],
        scratch_shapes=[pltpu.SemaphoreType.DMA((2,))],
        compiler_params=LITTLE,
        name="tables",
    )(in_hbm(jnp.asarray(window_table(), BF)), in_hbm(jnp.asarray(mix_table(), BF)))


def rotate_kernel(*refs):
    slots, (win_ref, mix_ref, out_ref) = refs[:N_XC], refs[N_XC:]
    member = lax.axis_index("x") * 2 + lax.axis_index("core")
    g = jnp.concatenate([unpack(ref[...]) for ref in slots], axis=0).astype(BF)
    window = win_ref[...]
    parts = []
    for j in range(N_Q):
        parts.append(
            jnp.dot(g[:, j * BLK : (j + 1) * BLK], window, preferred_element_type=F32)
        )
    spread = jnp.concatenate(parts, axis=0)
    lanes = lax.broadcasted_iota(jnp.int32, (LANE, LANE), 1)
    halves = []
    for z in range(2):
        start = ROWS * (member + N_XC * z)
        both = split_dot(
            mix_ref[z * 2 * LANE : (z + 1) * 2 * LANE, :], spread[:, z * LANE : (z + 1) * LANE]
        )
        wrapped = start % BLK + lanes >= BLK
        mixed = jnp.where(wrapped, both[LANE:], both[:LANE])
        halves.append(mixed.reshape(N_TOK, 1, GROUP, LANE))
    out_ref[...] = jnp.concatenate(halves, axis=1).reshape(2 * LANE, LANE)


def rotate(slots, window, mix):
    return pl.pallas_call(
        rotate_kernel,
        in_specs=[VMEM] * (N_XC + 2),
        out_specs=VMEM,
        out_shape=jax.ShapeDtypeStruct((2 * LANE, LANE), F32),
        compiler_params=LITTLE,
        name="rotate",
    )(*slots, window, mix)


def finish_kernel(x_ref, h_ref, out_ref):
    terms = x_ref[...].reshape(N_TOK, 2, GROUP, LANE)
    total = (terms[:, 0] + terms[:, 1]).reshape(COLS, LANE) * (1.0 / (FF * TOKENS))
    dims = (((0,), (0,)), ((), ()))
    dot = functools.partial(lax.dot_general, dimension_numbers=dims, preferred_element_type=F32)
    high = total.astype(BF)
    rest = total - high.astype(F32)
    mid = rest.astype(BF)
    low = (rest - mid.astype(F32)).astype(BF)
    table = h_ref[...]
    result = dot(high, table) + (dot(mid, table) + dot(low, table))
    out_ref[...] = result[:ROWS]


def finish(x, table):
    return pl.pallas_call(
        finish_kernel,
        in_specs=[VMEM, VMEM],
        out_specs=VMEM,
        out_shape=jax.ShapeDtypeStruct((ROWS, COLS), F32),
        compiler_params=LITTLE,
        name="finish",
    )(x, table)


def shift(x, axis, s):
    return lax.ppermute(x, axis, [(i, (i + s) % RING) for i in range(RING)])


def swap(x, axis):
    return lax.ppermute(x, axis, [(0, 1), (1, 0)])


def body(hidden, signs):
    send, keep, held, sign = fold(hidden, signs.reshape(N_L, LANE))
    pair, short = sum_core(keep, swap(send, "core"))
    mine = sum_x(pair, [shift(short, "x", s) for s in (1, 2, 3)])
    mine_z = swap(mine, "zh")
    acc = outer(mine, swap(mine, "core"), held)
    acc = outer_mine(mine_z, acc, held)
    own, *sends = outer_other(swap(mine_z, "core"), acc, held)

    own, *sends = sum_y(own, [shift(x, "y", s + 1) for s, x in enumerate(sends)])
    g = sum_z(own, [shift(x, "zl", s + 1) for s, x in enumerate(sends)], sign)

    ring = [g] + [shift(g, "x", s) for s in (1, 2, 3)]
    slots = [part for x in ring for part in (x, swap(x, "core"))]
    turned = rotate(slots, *tables())
    turned = lax.all_to_all(turned, ("y", "zl", "zh"), split_axis=0, concat_axis=0, tiled=True)
    return finish(turned, jnp.asarray(sylvester(COLS), BF))


def solution(mesh):
    fine = Mesh(mesh.devices.reshape(4, 4, 2, 4, 2), ("y", "zl", "zh", "x", "core"))
    return jax.shard_map(
        body,
        mesh=fine,
        in_specs=(P(TOK_AXES, TP_AXES), P(TP_AXES)),
        out_specs=P(TOK_AXES + TP_AXES, None),
        check_vma=False,
    )
```

time: 102 us -> 76.8 us (0.75)
  blocking collectives: 48.8 us -> 18.6 us
  starting transfers between devices: 16.8 us -> 37.7 us
  Pallas kernels: 18.7 us -> 6.62 us
  other arithmetic: 3.62 us -> 0 us
  waiting for transfers between devices: 11.2 us -> 13.6 us
  local copies, waits for them, and re-layouts: 1.95 us -> 0.01 us
    all_to_all x2 -> x0, blocking collectives: 33.5 us -> none  [the longest x1 21.2 us: body(): lax.all_to_all(wide, TOK_AXES, split_axis=0, concat_axis=0, tiled=True)]
    ppermute x6 -> x20, starting transfers between devices: 16.8 us -> 37.7 us  [the longest x8 19.8 us: swap(): return lax.ppermute(x, axis, [(0, 1), (1, 0)])]
    pallas_call x5 -> x11, Pallas kernels: 18.7 us -> 6.62 us  [the longest x1 2.17 us: fold(): pl.pallas_call(fold_kernel, in_specs=[HBM, HBM], out_specs=[VMEM] * 4, ou...]
    all_to_all x1, blocking collectives: 15.3 us -> 18.6 us  [body(): lax.all_to_all(turned, ('y', 'zl', 'zh'), split_axis=0, concat_axis=0, ti...]
    convert_element_type x3 -> x0, other arithmetic: 3.01 us -> none  [the longest x1 1.02 us: body(): mine = total.astype(BF)]
    ppermute x6 -> x20, waiting for transfers between devices: 11.2 us -> 13.6 us  [the longest x12 11.6 us: shift(): return lax.ppermute(x, axis, [(i, (i + s) % RING) for i in range(RING)])]
    reshape x1 -> x0, local copies, waits for them, and re-layouts: 1.29 us -> none  [body(): signs = signs.reshape(1, WIDTH)]
  transfers between devices with their start and end apart: 6 -> 20, of which waited for: 4 -> 9; matrix products, arithmetic and copies ran while one was open for 0% -> 0% of each run, Pallas kernels for 0% -> 3%
where the time goes in v2:
time: 76.8 us; the launch traced here: 76.6 us
  starting transfers between devices  37.7 us (49%)
  blocking collectives  18.6 us (24%)
  waiting for transfers between devices  13.6 us (18%)
  Pallas kernels  6.62 us (9%)
    ppermute x8, starting transfers between devices, swap(): return lax.ppermute(x, axis, [(0, 1), (1, 0)])  19.8 us
    all_to_all x1, blocking collectives, body(): lax.all_to_all(turned, ('y', 'zl', 'zh'), split_axis=0, concat_axis=0, ti...  18.6 us
    ppermute x12, starting transfers between devices, shift(): return lax.ppermute(x, axis, [(i, (i + s) % RING) for i in range(RING)])  17.9 us
    ppermute x12, waiting for transfers between devices, shift(): return lax.ppermute(x, axis, [(i, (i + s) % RING) for i in range(RING)])  11.6 us
    pallas_call x1, Pallas kernels, fold(): pl.pallas_call(fold_kernel, in_specs=[HBM, HBM], out_specs=[VMEM] * 4, ou...  2.17 us
    ppermute x8, waiting for transfers between devices, swap(): return lax.ppermute(x, axis, [(0, 1), (1, 0)])  1.99 us
  transfers between devices with their start and end apart: 20, of which 9 were waited for; matrix products, arithmetic and copies ran while one was open for 0% of the time, Pallas kernels for 3%

profile of v2, /device:TPU:1, one launch (start us, length us, event | category | flops | bytes accessed | tf_op | source)
XLA Modules:
  0.0 76.6 jit_solution(15246974514079202564)
XLA Ops:
  0.0 2.2 %fold.1 = (bf16[512,128]{1,0:T(8,128)(2,1)S(1)}, f32[512,128]{1,0:T(8,128)S(1)}, bf16[1024,1792]{1,0:T(8,128)(2,1)S(1)}, f32[14,128]{1,0:T(8,128)S(1)}) custom-call(bf16[1024,1792]{1,0:T(8,128)(2,1)} %x_ref.1, s32[14,128]{1,0:T(8,128)} %bitcast.5), custom_call_target="tpu_custom_call" | custom-call | flops 3670016 | bytes 3670016 | tf_op jit(solution)/shard_map/fold/pallas_call | solution.py:143
  2.2 3.3 %collective-permute-start = (bf16[512,128]{1,0:T(8,128)(2,1)S(1)}, bf16[512,128]{1,0:T(8,128)(2,1)S(1)}, u32[]{:S(2)}, u32[]{:S(2)}) collective-permute-start(bf16[512,128]{1,0:T(8,128)(2,1)S(1)} %get-tuple-element.22), channel_id=1, source_target_pairs={{0,1},{1,0},{2,3},{3,2},{4,5},{5,4},{6,7},{7,6},{8,9},{9,8},{10,11... | collective-permute-start | bytes 393224 | tf_op jit(solution)/shard_map/ppermute | solution.py:434
  5.5 1.0 %collective-permute-done.a = bf16[512,128]{1,0:T(8,128)(2,1)S(1)} collective-permute-done((bf16[512,128]{1,0:T(8,128)(2,1)S(1)}, bf16[512,128]{1,0:T(8,128)(2,1)S(1)}, u32[]{:S(2)}, u32[]{:S(2)}) %collective-permute-start) | collective-permute-done | bytes 131104 | tf_op jit(solution)/shard_map/ppermute | solution.py:434
  6.5 0.1 collective-permute-start.1
  6.6 1.9 %collective-permute-start.2 = (bf16[512,128]{1,0:T(8,128)(2,1)S(1)}, bf16[512,128]{1,0:T(8,128)(2,1)S(1)}, u32[]{:S(2)}, u32[]{:S(2)}) collective-permute-start(bf16[512,128]{1,0:T(8,128)(2,1)S(1)} %get-tuple-element.24), channel_id=1, source_target_pairs={{0,4},{2,6},{4,0},{6,2},{1,5},{3,7},{5,1},{7,3},{8,12},{10,14},{12... | collective-permute-start | bytes 393224 | tf_op jit(solution)/shard_map/ppermute | solution.py:430
  8.5 1.2 %collective-permute-start.3 = (bf16[512,128]{1,0:T(8,128)(2,1)S(1)}, bf16[512,128]{1,0:T(8,128)(2,1)S(1)}, u32[]{:S(2)}, u32[]{:S(2)}) collective-permute-start(bf16[512,128]{1,0:T(8,128)(2,1)S(1)} %get-tuple-element.24), channel_id=1, source_target_pairs={{0,6},{2,0},{4,2},{6,4},{1,7},{3,1},{5,3},{7,5},{8,14},{10,8},{12,... | collective-permute-start | bytes 393224 | tf_op jit(solution)/shard_map/ppermute | solution.py:430
  9.7 3.6 %collective-permute-done.1.a = bf16[512,128]{1,0:T(8,128)(2,1)S(1)} collective-permute-done((bf16[512,128]{1,0:T(8,128)(2,1)S(1)}, bf16[512,128]{1,0:T(8,128)(2,1)S(1)}, u32[]{:S(2)}, u32[]{:S(2)}) %collective-permute-start.1) | collective-permute-done | bytes 131104 | tf_op jit(solution)/shard_map/ppermute | solution.py:430
  13.3 1.4 %collective-permute-done.2.b = bf16[512,128]{1,0:T(8,128)(2,1)S(1)} collective-permute-done((bf16[512,128]{1,0:T(8,128)(2,1)S(1)}, bf16[512,128]{1,0:T(8,128)(2,1)S(1)}, u32[]{:S(2)}, u32[]{:S(2)}) %collective-permute-start.2) | collective-permute-done | bytes 131104 | tf_op jit(solution)/shard_map/ppermute | solution.py:430
  14.7 1.0 %collective-permute-done.3.c = bf16[512,128]{1,0:T(8,128)(2,1)S(1)} collective-permute-done((bf16[512,128]{1,0:T(8,128)(2,1)S(1)}, bf16[512,128]{1,0:T(8,128)(2,1)S(1)}, u32[]{:S(2)}, u32[]{:S(2)}) %collective-permute-start.3) | collective-permute-done | bytes 131104 | tf_op jit(solution)/shard_map/ppermute | solution.py:430
  15.6 0.1 sum_x.1.mine
  15.8 6.0 %collective-permute-start.4 = (bf16[128,512]{1,0:T(8,128)(2,1)S(1)}, bf16[128,512]{1,0:T(8,128)(2,1)S(1)}, u32[]{:S(2)}, u32[]{:S(2)}) collective-permute-start(bf16[128,512]{1,0:T(8,128)(2,1)S(1)} %sum_x.1.mine), channel_id=1, source_target_pairs={{0,8},{8,0},{1,9},{9,1},{2,10},{10,2},{3,11},{11,3},{4,12},{12,4},... | collective-permute-start | bytes 393224 | tf_op jit(solution)/shard_map/ppermute | solution.py:434
  21.7 1.5 %collective-permute-start.6 = (bf16[128,512]{1,0:T(8,128)(2,1)S(1)}, bf16[128,512]{1,0:T(8,128)(2,1)S(1)}, u32[]{:S(2)}, u32[]{:S(2)}) collective-permute-start(bf16[128,512]{1,0:T(8,128)(2,1)S(1)} %sum_x.1.mine), channel_id=1, source_target_pairs={{0,1},{1,0},{2,3},{3,2},{4,5},{5,4},{6,7},{7,6},{8,9},{9,8},{10,11... | collective-permute-start | bytes 393224 | tf_op jit(solution)/shard_map/ppermute | solution.py:434
  23.2 1.0 %collective-permute-done.4.mine = bf16[128,512]{1,0:T(8,128)(2,1)S(1)} collective-permute-done((bf16[128,512]{1,0:T(8,128)(2,1)S(1)}, bf16[128,512]{1,0:T(8,128)(2,1)S(1)}, u32[]{:S(2)}, u32[]{:S(2)}) %collective-permute-start.4) | collective-permute-done | bytes 131104 | tf_op jit(solution)/shard_map/ppermute | solution.py:434
  24.2 3.6 %collective-permute-start.5 = (bf16[128,512]{1,0:T(8,128)(2,1)S(1)}, bf16[128,512]{1,0:T(8,128)(2,1)S(1)}, u32[]{:S(2)}, u32[]{:S(2)}) collective-permute-start(bf16[128,512]{1,0:T(8,128)(2,1)S(1)} %collective-permute-done.4.mine), channel_id=1, source_target_pairs={{0,1},{1,0},{2,3},{3,2},{4,5},{5,4},{6,7},{7,6},{8,9},{9,8},{10,11... | collective-permute-start | bytes 393224 | tf_op jit(solution)/shard_map/ppermute | solution.py:434
  27.8 0.0 collective-permute-done.6.other
  27.8 0.6 outer.1.acc_ref
  28.5 0.4 outer_mine.1.acc_ref
  28.9 0.0 collective-permute-done.5.other
  28.9 0.5 outer_other.1
  29.4 1.4 %collective-permute-start.7 = (bf16[32,1792]{1,0:T(8,128)(2,1)S(1)}, bf16[32,1792]{1,0:T(8,128)(2,1)S(1)}, u32[]{:S(2)}, u32[]{:S(2)}) collective-permute-start(bf16[32,1792]{1,0:T(8,128)(2,1)S(1)} %get-tuple-element.27), channel_id=1, source_target_pairs={{0,64},{64,128},{128,192},{192,0},{1,65},{65,129},{129,193},{193,1... | collective-permute-start | bytes 344072 | tf_op jit(solution)/shard_map/ppermute | solution.py:430
  30.7 2.6 %collective-permute-start.8 = (bf16[32,1792]{1,0:T(8,128)(2,1)S(1)}, bf16[32,1792]{1,0:T(8,128)(2,1)S(1)}, u32[]{:S(2)}, u32[]{:S(2)}) collective-permute-start(bf16[32,1792]{1,0:T(8,128)(2,1)S(1)} %get-tuple-element.28), channel_id=1, source_target_pairs={{0,128},{64,192},{128,0},{192,64},{1,129},{65,193},{129,1},{193,65... | collective-permute-start | bytes 344072 | tf_op jit(solution)/shard_map/ppermute | solution.py:430
  33.4 1.1 %collective-permute-start.9 = (bf16[32,1792]{1,0:T(8,128)(2,1)S(1)}, bf16[32,1792]{1,0:T(8,128)(2,1)S(1)}, u32[]{:S(2)}, u32[]{:S(2)}) collective-permute-start(bf16[32,1792]{1,0:T(8,128)(2,1)S(1)} %get-tuple-element.29), channel_id=1, source_target_pairs={{0,192},{64,0},{128,64},{192,128},{1,193},{65,1},{129,65},{193,129... | collective-permute-start | bytes 344072 | tf_op jit(solution)/shard_map/ppermute | solution.py:430
  34.4 0.9 %collective-permute-done.7.a = bf16[32,1792]{1,0:T(8,128)(2,1)S(1)} collective-permute-done((bf16[32,1792]{1,0:T(8,128)(2,1)S(1)}, bf16[32,1792]{1,0:T(8,128)(2,1)S(1)}, u32[]{:S(2)}, u32[]{:S(2)}) %collective-permute-start.7) | collective-permute-done | bytes 114720 | tf_op jit(solution)/shard_map/ppermute | solution.py:430
  35.3 3.6 %collective-permute-done.8.b = bf16[32,1792]{1,0:T(8,128)(2,1)S(1)} collective-permute-done((bf16[32,1792]{1,0:T(8,128)(2,1)S(1)}, bf16[32,1792]{1,0:T(8,128)(2,1)S(1)}, u32[]{:S(2)}, u32[]{:S(2)}) %collective-permute-start.8) | collective-permute-done | bytes 114720 | tf_op jit(solution)/shard_map/ppermute | solution.py:430
  38.9 0.0 collective-permute-done.9.c
  38.9 0.1 sum_y.1
  38.9 2.1 %collective-permute-start.10 = (bf16[16,896]{1,0:T(8,128)(2,1)S(1)}, bf16[16,896]{1,0:T(8,128)(2,1)S(1)}, u32[]{:S(2)}, u32[]{:S(2)}) collective-permute-start(bf16[16,896]{1,0:T(8,128)(2,1)S(1)} %get-tuple-element.31), channel_id=1, source_target_pairs={{0,16},{16,32},{32,48},{48,0},{1,17},{17,33},{33,49},{49,1},{2,18}... | collective-permute-start | bytes 86024 | tf_op jit(solution)/shard_map/ppermute | solution.py:430
  41.0 0.9 %collective-permute-start.11 = (bf16[16,896]{1,0:T(8,128)(2,1)S(1)}, bf16[16,896]{1,0:T(8,128)(2,1)S(1)}, u32[]{:S(2)}, u32[]{:S(2)}) collective-permute-start(bf16[16,896]{1,0:T(8,128)(2,1)S(1)} %get-tuple-element.32), channel_id=1, source_target_pairs={{0,32},{16,48},{32,0},{48,16},{1,33},{17,49},{33,1},{49,17},{2,34}... | collective-permute-start | bytes 86024 | tf_op jit(solution)/shard_map/ppermute | solution.py:430
  41.9 2.3 %collective-permute-start.12 = (bf16[16,896]{1,0:T(8,128)(2,1)S(1)}, bf16[16,896]{1,0:T(8,128)(2,1)S(1)}, u32[]{:S(2)}, u32[]{:S(2)}) collective-permute-start(bf16[16,896]{1,0:T(8,128)(2,1)S(1)} %get-tuple-element.33), channel_id=1, source_target_pairs={{0,48},{16,0},{32,16},{48,32},{1,49},{17,1},{33,17},{49,33},{2,50}... | collective-permute-start | bytes 86024 | tf_op jit(solution)/shard_map/ppermute | solution.py:430
  44.1 0.0 collective-permute-done.10.a
  44.1 0.8 %collective-permute-done.11.b = bf16[16,896]{1,0:T(8,128)(2,1)S(1)} collective-permute-done((bf16[16,896]{1,0:T(8,128)(2,1)S(1)}, bf16[16,896]{1,0:T(8,128)(2,1)S(1)}, u32[]{:S(2)}, u32[]{:S(2)}) %collective-permute-start.11) | collective-permute-done | bytes 28704 | tf_op jit(solution)/shard_map/ppermute | solution.py:430
  44.9 0.4 collective-permute-done.12.c
  45.4 0.0 copy-start
  45.4 1.1 %collective-permute-start.14 = (bf16[16,896]{1,0:T(8,128)(2,1)S(1)}, bf16[16,896]{1,0:T(8,128)(2,1)S(1)}, u32[]{:S(2)}, u32[]{:S(2)}) collective-permute-start(bf16[16,896]{1,0:T(8,128)(2,1)S(1)} %sum_z.1.refs_0_), channel_id=1, source_target_pairs={{0,2},{2,4},{4,6},{6,0},{1,3},{3,5},{5,7},{7,1},{8,10},{10,12},{12... | collective-permute-start | bytes 86024 | tf_op jit(solution)/shard_map/ppermute | solution.py:430
  46.5 2.1 %collective-permute-start.16 = (bf16[16,896]{1,0:T(8,128)(2,1)S(1)}, bf16[16,896]{1,0:T(8,128)(2,1)S(1)}, u32[]{:S(2)}, u32[]{:S(2)}) collective-permute-start(bf16[16,896]{1,0:T(8,128)(2,1)S(1)} %sum_z.1.refs_0_), channel_id=1, source_target_pairs={{0,4},{2,6},{4,0},{6,2},{1,5},{3,7},{5,1},{7,3},{8,12},{10,14},{12... | collective-permute-start | bytes 86024 | tf_op jit(solution)/shard_map/ppermute | solution.py:430
  48.6 1.2 %collective-permute-start.18 = (bf16[16,896]{1,0:T(8,128)(2,1)S(1)}, bf16[16,896]{1,0:T(8,128)(2,1)S(1)}, u32[]{:S(2)}, u32[]{:S(2)}) collective-permute-start(bf16[16,896]{1,0:T(8,128)(2,1)S(1)} %sum_z.1.refs_0_), channel_id=1, source_target_pairs={{0,6},{2,0},{4,2},{6,4},{1,7},{3,1},{5,3},{7,5},{8,14},{10,8},{12,... | collective-permute-start | bytes 86024 | tf_op jit(solution)/shard_map/ppermute | solution.py:430
  49.9 3.2 %collective-permute-start.13 = (bf16[16,896]{1,0:T(8,128)(2,1)S(1)}, bf16[16,896]{1,0:T(8,128)(2,1)S(1)}, u32[]{:S(2)}, u32[]{:S(2)}) collective-permute-start(bf16[16,896]{1,0:T(8,128)(2,1)S(1)} %sum_z.1.refs_0_), channel_id=1, source_target_pairs={{0,1},{1,0},{2,3},{3,2},{4,5},{5,4},{6,7},{7,6},{8,9},{9,8},{10,11... | collective-permute-start | bytes 86024 | tf_op jit(solution)/shard_map/ppermute | solution.py:434
  53.0 0.0 collective-permute-done.14.refs_2_
  53.0 0.0 collective-permute-start.15
  53.0 0.0 collective-permute-done.16.refs_4_
  53.1 1.3 %collective-permute-start.17 = (bf16[16,896]{1,0:T(8,128)(2,1)S(1)}, bf16[16,896]{1,0:T(8,128)(2,1)S(1)}, u32[]{:S(2)}, u32[]{:S(2)}) collective-permute-start(bf16[16,896]{1,0:T(8,128)(2,1)S(1)} %collective-permute-done.16.refs_4_), channel_id=1, source_target_pairs={{0,1},{1,0},{2,3},{3,2},{4,5},{5,4},{6,7},{7,6},{8,9},{9,8},{10,11... | collective-permute-start | bytes 86024 | tf_op jit(solution)/shard_map/ppermute | solution.py:434
  54.4 0.0 collective-permute-done.18.refs_6_
  54.4 1.0 %collective-permute-start.19 = (bf16[16,896]{1,0:T(8,128)(2,1)S(1)}, bf16[16,896]{1,0:T(8,128)(2,1)S(1)}, u32[]{:S(2)}, u32[]{:S(2)}) collective-permute-start(bf16[16,896]{1,0:T(8,128)(2,1)S(1)} %collective-permute-done.18.refs_6_), channel_id=1, source_target_pairs={{0,1},{1,0},{2,3},{3,2},{4,5},{5,4},{6,7},{7,6},{8,9},{9,8},{10,11... | collective-permute-start | bytes 86024 | tf_op jit(solution)/shard_map/ppermute | solution.py:434
  55.4 1.1 %tables.1 = (bf16[256,256]{1,0:T(8,128)(2,1)S(1)}, bf16[512,448]{1,0:T(8,128)(2,1)S(1)}) custom-call(bf16[8,256,256]{2,1,0:T(8,128)(2,1)} %constant.6.clone.win_hbm, bf16[16,512,448]{2,1,0:T(8,128)(2,1)} %constant.7.clone.mix_hbm), custom_call_target="tpu_custom_call" | custom-call | tf_op jit(solution)/shard_map/tables/pallas_call | solution.py:355
  56.5 0.0 collective-permute-done.13.refs_1_
  56.5 0.0 collective-permute-done.15.refs_3_
  56.5 0.0 collective-permute-done.17.refs_5_
  56.5 0.0 collective-permute-done.19.refs_7_
  56.5 0.7 rotate.1
  57.2 18.6 %all_to_all.11 = f32[32,8,128]{2,1,0:T(8,128)S(1)} all-to-all(f32[32,8,128]{2,1,0:T(8,128)S(1)} %bitcast.4), channel_id=1, replica_groups=mesh['y'=4,'zl'=4,'zh'=2,'x'=4,'core'=2] {'y','zl','zh'}, dimensions={0} | all-to-all | bytes 262144 | tf_op jit(solution)/shard_map/all_to_all | solution.py:452
  75.8 0.0 copy-done
  75.8 0.8 %finish.1 = f32[112,128]{1,0:T(8,128)} custom-call(f32[256,128]{1,0:T(8,128)S(1)} %bitcast.3, bf16[128,128]{1,0:T(8,128)(2,1)S(1)} %copy-done), custom_call_target="tpu_custom_call" | custom-call | tf_op jit(solution)/shard_map/finish/pallas_call | solution.py:419
  (2 shorter events, 0.1 us)
Async XLA Ops:
  2.2 4.3 %collective-permute-start = (bf16[512,128]{1,0:T(8,128)(2,1)S(1)}, bf16[512,128]{1,0:T(8,128)(2,1)S(1)}, u32[]{:S(2)}, u32[]{:S(2)}) collective-permute-start(bf16[512,128]{1,0:T(8,128)(2,1)S(1)} %get-tuple-element.22), channel_id=1, source_target_pairs={{0,1},{1,0},{2,3},{3,2},{4,5},{5,4},{6,7},{7,6},{8,9},{9,8},{10,11... | collective-permute-start | bytes 393224 | tf_op jit(solution)/shard_map/ppermute | solution.py:434
  6.5 6.8 %collective-permute-start.1 = (bf16[512,128]{1,0:T(8,128)(2,1)S(1)}, bf16[512,128]{1,0:T(8,128)(2,1)S(1)}, u32[]{:S(2)}, u32[]{:S(2)}) collective-permute-start(bf16[512,128]{1,0:T(8,128)(2,1)S(1)} %get-tuple-element.24), channel_id=1, source_target_pairs={{0,2},{2,4},{4,6},{6,0},{1,3},{3,5},{5,7},{7,1},{8,10},{10,12},{12... | collective-permute-start | bytes 393224 | tf_op jit(solution)/shard_map/ppermute | solution.py:430
  6.6 8.0 %collective-permute-start.2 = (bf16[512,128]{1,0:T(8,128)(2,1)S(1)}, bf16[512,128]{1,0:T(8,128)(2,1)S(1)}, u32[]{:S(2)}, u32[]{:S(2)}) collective-permute-start(bf16[512,128]{1,0:T(8,128)(2,1)S(1)} %get-tuple-element.24), channel_id=1, source_target_pairs={{0,4},{2,6},{4,0},{6,2},{1,5},{3,7},{5,1},{7,3},{8,12},{10,14},{12... | collective-permute-start | bytes 393224 | tf_op jit(solution)/shard_map/ppermute | solution.py:430
  8.5 7.1 %collective-permute-start.3 = (bf16[512,128]{1,0:T(8,128)(2,1)S(1)}, bf16[512,128]{1,0:T(8,128)(2,1)S(1)}, u32[]{:S(2)}, u32[]{:S(2)}) collective-permute-start(bf16[512,128]{1,0:T(8,128)(2,1)S(1)} %get-tuple-element.24), channel_id=1, source_target_pairs={{0,6},{2,0},{4,2},{6,4},{1,7},{3,1},{5,3},{7,5},{8,14},{10,8},{12,... | collective-permute-start | bytes 393224 | tf_op jit(solution)/shard_map/ppermute | solution.py:430
  15.8 8.4 %collective-permute-start.4 = (bf16[128,512]{1,0:T(8,128)(2,1)S(1)}, bf16[128,512]{1,0:T(8,128)(2,1)S(1)}, u32[]{:S(2)}, u32[]{:S(2)}) collective-permute-start(bf16[128,512]{1,0:T(8,128)(2,1)S(1)} %sum_x.1.mine), channel_id=1, source_target_pairs={{0,8},{8,0},{1,9},{9,1},{2,10},{10,2},{3,11},{11,3},{4,12},{12,4},... | collective-permute-start | bytes 393224 | tf_op jit(solution)/shard_map/ppermute | solution.py:434
  21.7 6.1 %collective-permute-start.6 = (bf16[128,512]{1,0:T(8,128)(2,1)S(1)}, bf16[128,512]{1,0:T(8,128)(2,1)S(1)}, u32[]{:S(2)}, u32[]{:S(2)}) collective-permute-start(bf16[128,512]{1,0:T(8,128)(2,1)S(1)} %sum_x.1.mine), channel_id=1, source_target_pairs={{0,1},{1,0},{2,3},{3,2},{4,5},{5,4},{6,7},{7,6},{8,9},{9,8},{10,11... | collective-permute-start | bytes 393224 | tf_op jit(solution)/shard_map/ppermute | solution.py:434
  24.2 4.7 %collective-permute-start.5 = (bf16[128,512]{1,0:T(8,128)(2,1)S(1)}, bf16[128,512]{1,0:T(8,128)(2,1)S(1)}, u32[]{:S(2)}, u32[]{:S(2)}) collective-permute-start(bf16[128,512]{1,0:T(8,128)(2,1)S(1)} %collective-permute-done.4.mine), channel_id=1, source_target_pairs={{0,1},{1,0},{2,3},{3,2},{4,5},{5,4},{6,7},{7,6},{8,9},{9,8},{10,11... | collective-permute-start | bytes 393224 | tf_op jit(solution)/shard_map/ppermute | solution.py:434
  29.4 5.9 %collective-permute-start.7 = (bf16[32,1792]{1,0:T(8,128)(2,1)S(1)}, bf16[32,1792]{1,0:T(8,128)(2,1)S(1)}, u32[]{:S(2)}, u32[]{:S(2)}) collective-permute-start(bf16[32,1792]{1,0:T(8,128)(2,1)S(1)} %get-tuple-element.27), channel_id=1, source_target_pairs={{0,64},{64,128},{128,192},{192,0},{1,65},{65,129},{129,193},{193,1... | collective-permute-start | bytes 344072 | tf_op jit(solution)/shard_map/ppermute | solution.py:430
  30.7 8.1 %collective-permute-start.8 = (bf16[32,1792]{1,0:T(8,128)(2,1)S(1)}, bf16[32,1792]{1,0:T(8,128)(2,1)S(1)}, u32[]{:S(2)}, u32[]{:S(2)}) collective-permute-start(bf16[32,1792]{1,0:T(8,128)(2,1)S(1)} %get-tuple-element.28), channel_id=1, source_target_pairs={{0,128},{64,192},{128,0},{192,64},{1,129},{65,193},{129,1},{193,65... | collective-permute-start | bytes 344072 | tf_op jit(solution)/shard_map/ppermute | solution.py:430
  33.4 5.5 %collective-permute-start.9 = (bf16[32,1792]{1,0:T(8,128)(2,1)S(1)}, bf16[32,1792]{1,0:T(8,128)(2,1)S(1)}, u32[]{:S(2)}, u32[]{:S(2)}) collective-permute-start(bf16[32,1792]{1,0:T(8,128)(2,1)S(1)} %get-tuple-element.29), channel_id=1, source_target_pairs={{0,192},{64,0},{128,64},{192,128},{1,193},{65,1},{129,65},{193,129... | collective-permute-start | bytes 344072 | tf_op jit(solution)/shard_map/ppermute | solution.py:430
  38.9 5.2 %collective-permute-start.10 = (bf16[16,896]{1,0:T(8,128)(2,1)S(1)}, bf16[16,896]{1,0:T(8,128)(2,1)S(1)}, u32[]{:S(2)}, u32[]{:S(2)}) collective-permute-start(bf16[16,896]{1,0:T(8,128)(2,1)S(1)} %get-tuple-element.31), channel_id=1, source_target_pairs={{0,16},{16,32},{32,48},{48,0},{1,17},{17,33},{33,49},{49,1},{2,18}... | collective-permute-start | bytes 86024 | tf_op jit(solution)/shard_map/ppermute | solution.py:430
  41.0 3.9 %collective-permute-start.11 = (bf16[16,896]{1,0:T(8,128)(2,1)S(1)}, bf16[16,896]{1,0:T(8,128)(2,1)S(1)}, u32[]{:S(2)}, u32[]{:S(2)}) collective-permute-start(bf16[16,896]{1,0:T(8,128)(2,1)S(1)} %get-tuple-element.32), channel_id=1, source_target_pairs={{0,32},{16,48},{32,0},{48,16},{1,33},{17,49},{33,1},{49,17},{2,34}... | collective-permute-start | bytes 86024 | tf_op jit(solution)/shard_map/ppermute | solution.py:430
  41.9 3.5 %collective-permute-start.12 = (bf16[16,896]{1,0:T(8,128)(2,1)S(1)}, bf16[16,896]{1,0:T(8,128)(2,1)S(1)}, u32[]{:S(2)}, u32[]{:S(2)}) collective-permute-start(bf16[16,896]{1,0:T(8,128)(2,1)S(1)} %get-tuple-element.33), channel_id=1, source_target_pairs={{0,48},{16,0},{32,16},{48,32},{1,49},{17,1},{33,17},{49,33},{2,50}... | collective-permute-start | bytes 86024 | tf_op jit(solution)/shard_map/ppermute | solution.py:430
  45.4 30.4 %copy-start = (bf16[128,128]{1,0:T(8,128)(2,1)S(1)}, bf16[128,128]{1,0:T(8,128)(2,1)}, u32[]{:S(2)}) copy-start(bf16[128,128]{1,0:T(8,128)(2,1)} %constant.8.clone.h_ref) | copy-start | bytes 98308
  45.4 7.7 %collective-permute-start.14 = (bf16[16,896]{1,0:T(8,128)(2,1)S(1)}, bf16[16,896]{1,0:T(8,128)(2,1)S(1)}, u32[]{:S(2)}, u32[]{:S(2)}) collective-permute-start(bf16[16,896]{1,0:T(8,128)(2,1)S(1)} %sum_z.1.refs_0_), channel_id=1, source_target_pairs={{0,2},{2,4},{4,6},{6,0},{1,3},{3,5},{5,7},{7,1},{8,10},{10,12},{12... | collective-permute-start | bytes 86024 | tf_op jit(solution)/shard_map/ppermute | solution.py:430
  46.5 6.6 %collective-permute-start.16 = (bf16[16,896]{1,0:T(8,128)(2,1)S(1)}, bf16[16,896]{1,0:T(8,128)(2,1)S(1)}, u32[]{:S(2)}, u32[]{:S(2)}) collective-permute-start(bf16[16,896]{1,0:T(8,128)(2,1)S(1)} %sum_z.1.refs_0_), channel_id=1, source_target_pairs={{0,4},{2,6},{4,0},{6,2},{1,5},{3,7},{5,1},{7,3},{8,12},{10,14},{12... | collective-permute-start | bytes 86024 | tf_op jit(solution)/shard_map/ppermute | solution.py:430
  48.6 5.8 %collective-permute-start.18 = (bf16[16,896]{1,0:T(8,128)(2,1)S(1)}, bf16[16,896]{1,0:T(8,128)(2,1)S(1)}, u32[]{:S(2)}, u32[]{:S(2)}) collective-permute-start(bf16[16,896]{1,0:T(8,128)(2,1)S(1)} %sum_z.1.refs_0_), channel_id=1, source_target_pairs={{0,6},{2,0},{4,2},{6,4},{1,7},{3,1},{5,3},{7,5},{8,14},{10,8},{12,... | collective-permute-start | bytes 86024 | tf_op jit(solution)/shard_map/ppermute | solution.py:430
  49.9 6.6 %collective-permute-start.13 = (bf16[16,896]{1,0:T(8,128)(2,1)S(1)}, bf16[16,896]{1,0:T(8,128)(2,1)S(1)}, u32[]{:S(2)}, u32[]{:S(2)}) collective-permute-start(bf16[16,896]{1,0:T(8,128)(2,1)S(1)} %sum_z.1.refs_0_), channel_id=1, source_target_pairs={{0,1},{1,0},{2,3},{3,2},{4,5},{5,4},{6,7},{7,6},{8,9},{9,8},{10,11... | collective-permute-start | bytes 86024 | tf_op jit(solution)/shard_map/ppermute | solution.py:434
  53.0 3.5 %collective-permute-start.15 = (bf16[16,896]{1,0:T(8,128)(2,1)S(1)}, bf16[16,896]{1,0:T(8,128)(2,1)S(1)}, u32[]{:S(2)}, u32[]{:S(2)}) collective-permute-start(bf16[16,896]{1,0:T(8,128)(2,1)S(1)} %collective-permute-done.14.refs_2_), channel_id=1, source_target_pairs={{0,1},{1,0},{2,3},{3,2},{4,5},{5,4},{6,7},{7,6},{8,9},{9,8},{10,11... | collective-permute-start | bytes 86024 | tf_op jit(solution)/shard_map/ppermute | solution.py:434
  53.1 3.5 %collective-permute-start.17 = (bf16[16,896]{1,0:T(8,128)(2,1)S(1)}, bf16[16,896]{1,0:T(8,128)(2,1)S(1)}, u32[]{:S(2)}, u32[]{:S(2)}) collective-permute-start(bf16[16,896]{1,0:T(8,128)(2,1)S(1)} %collective-permute-done.16.refs_4_), channel_id=1, source_target_pairs={{0,1},{1,0},{2,3},{3,2},{4,5},{5,4},{6,7},{7,6},{8,9},{9,8},{10,11... | collective-permute-start | bytes 86024 | tf_op jit(solution)/shard_map/ppermute | solution.py:434
  54.4 2.1 %collective-permute-start.19 = (bf16[16,896]{1,0:T(8,128)(2,1)S(1)}, bf16[16,896]{1,0:T(8,128)(2,1)S(1)}, u32[]{:S(2)}, u32[]{:S(2)}) collective-permute-start(bf16[16,896]{1,0:T(8,128)(2,1)S(1)} %collective-permute-done.18.refs_6_), channel_id=1, source_target_pairs={{0,1},{1,0},{2,3},{3,2},{4,5},{5,4},{6,7},{7,6},{8,9},{9,8},{10,11... | collective-permute-start | bytes 86024 | tf_op jit(solution)/shard_map/ppermute | solution.py:434

commit v3 on v2

--- a/solution.py
+++ b/solution.py
@@ -437,13 +437,13 @@
 def body(hidden, signs):
     send, keep, held, sign = fold(hidden, signs.reshape(N_L, LANE))
     pair, short = sum_core(keep, swap(send, "core"))
-    mine = sum_x(pair, [shift(short, "x", s) for s in (1, 2, 3)])
+    mine = sum_x(pair, [shift(short, "x", s) for s in (1, 3, 2)])
     mine_z = swap(mine, "zh")
     acc = outer(mine, swap(mine, "core"), held)
     acc = outer_mine(mine_z, acc, held)
     own, *sends = outer_other(swap(mine_z, "core"), acc, held)
 
-    own, *sends = sum_y(own, [shift(x, "y", s + 1) for s, x in enumerate(sends)])
+    own, *sends = sum_y(own, [shift(sends[s - 1], "y", s) for s in (1, 3, 2)])
     g = sum_z(own, [shift(x, "zl", s + 1) for s, x in enumerate(sends)], sign)
 
     ring = [g] + [shift(g, "x", s) for s in (1, 2, 3)]

time: 76.8 us -> 75.4 us (0.982)
  blocking collectives: 18.6 us -> 17.4 us
    ppermute x12, starting transfers between devices: 17.9 us -> 15.8 us  [shift(): return lax.ppermute(x, axis, [(i, (i + s) % RING) for i in range(RING)])]
    ppermute x8, starting transfers between devices: 19.8 us -> 21.6 us  [swap(): return lax.ppermute(x, axis, [(0, 1), (1, 0)])]
    all_to_all x1, blocking collectives: 18.6 us -> 17.4 us  [body(): lax.all_to_all(turned, ('y', 'zl', 'zh'), split_axis=0, concat_axis=0, ti...]
where the time goes in v3:
time: 75.4 us; the launch traced here: 75.2 us
  starting transfers between devices  37.5 us (50%)
  blocking collectives  17.4 us (23%)
  waiting for transfers between devices  13.6 us (18%)
  Pallas kernels  6.62 us (9%)
    ppermute x8, starting transfers between devices, swap(): return lax.ppermute(x, axis, [(0, 1), (1, 0)])  21.6 us
    all_to_all x1, blocking collectives, body(): lax.all_to_all(turned, ('y', 'zl', 'zh'), split_axis=0, concat_axis=0, ti...  17.4 us
    ppermute x12, starting transfers between devices, shift(): return lax.ppermute(x, axis, [(i, (i + s) % RING) for i in range(RING)])  15.8 us
    ppermute x12, waiting for transfers between devices, shift(): return lax.ppermute(x, axis, [(i, (i + s) % RING) for i in range(RING)])  11.6 us
    pallas_call x1, Pallas kernels, fold(): pl.pallas_call(fold_kernel, in_specs=[HBM, HBM], out_specs=[VMEM] * 4, ou...  2.17 us
    ppermute x8, waiting for transfers between devices, swap(): return lax.ppermute(x, axis, [(0, 1), (1, 0)])  1.99 us
  transfers between devices with their start and end apart: 20, of which 9 were waited for; matrix products, arithmetic and copies ran while one was open for 0% of the time, Pallas kernels for 3%

profile of v3, /device:TPU:1, one launch (start us, length us, event | category | flops | bytes accessed | tf_op | source)
XLA Modules:
  0.0 75.2 jit_solution(10398424314724895852)
XLA Ops:
  0.0 2.2 %fold.1 = (bf16[512,128]{1,0:T(8,128)(2,1)S(1)}, f32[512,128]{1,0:T(8,128)S(1)}, bf16[1024,1792]{1,0:T(8,128)(2,1)S(1)}, f32[14,128]{1,0:T(8,128)S(1)}) custom-call(bf16[1024,1792]{1,0:T(8,128)(2,1)} %x_ref.1, s32[14,128]{1,0:T(8,128)} %bitcast.5), custom_call_target="tpu_custom_call" | custom-call | flops 3670016 | bytes 3670016 | tf_op jit(solution)/shard_map/fold/pallas_call | solution.py:143
  2.2 3.3 %collective-permute-start = (bf16[512,128]{1,0:T(8,128)(2,1)S(1)}, bf16[512,128]{1,0:T(8,128)(2,1)S(1)}, u32[]{:S(2)}, u32[]{:S(2)}) collective-permute-start(bf16[512,128]{1,0:T(8,128)(2,1)S(1)} %get-tuple-element.22), channel_id=1, source_target_pairs={{0,1},{1,0},{2,3},{3,2},{4,5},{5,4},{6,7},{7,6},{8,9},{9,8},{10,11... | collective-permute-start | bytes 393224 | tf_op jit(solution)/shard_map/ppermute | solution.py:434
  5.5 1.0 %collective-permute-done.a = bf16[512,128]{1,0:T(8,128)(2,1)S(1)} collective-permute-done((bf16[512,128]{1,0:T(8,128)(2,1)S(1)}, bf16[512,128]{1,0:T(8,128)(2,1)S(1)}, u32[]{:S(2)}, u32[]{:S(2)}) %collective-permute-start) | collective-permute-done | bytes 131104 | tf_op jit(solution)/shard_map/ppermute | solution.py:434
  6.5 0.1 collective-permute-start.1
  6.6 2.7 %collective-permute-start.2 = (bf16[512,128]{1,0:T(8,128)(2,1)S(1)}, bf16[512,128]{1,0:T(8,128)(2,1)S(1)}, u32[]{:S(2)}, u32[]{:S(2)}) collective-permute-start(bf16[512,128]{1,0:T(8,128)(2,1)S(1)} %get-tuple-element.24), channel_id=1, source_target_pairs={{0,6},{2,0},{4,2},{6,4},{1,7},{3,1},{5,3},{7,5},{8,14},{10,8},{12,... | collective-permute-start | bytes 393224 | tf_op jit(solution)/shard_map/ppermute | solution.py:430
  9.3 0.0 collective-permute-start.3
  9.3 3.3 %collective-permute-done.1.a = bf16[512,128]{1,0:T(8,128)(2,1)S(1)} collective-permute-done((bf16[512,128]{1,0:T(8,128)(2,1)S(1)}, bf16[512,128]{1,0:T(8,128)(2,1)S(1)}, u32[]{:S(2)}, u32[]{:S(2)}) %collective-permute-start.1) | collective-permute-done | bytes 131104 | tf_op jit(solution)/shard_map/ppermute | solution.py:430
  12.5 1.9 %collective-permute-done.2.b = bf16[512,128]{1,0:T(8,128)(2,1)S(1)} collective-permute-done((bf16[512,128]{1,0:T(8,128)(2,1)S(1)}, bf16[512,128]{1,0:T(8,128)(2,1)S(1)}, u32[]{:S(2)}, u32[]{:S(2)}) %collective-permute-start.2) | collective-permute-done | bytes 131104 | tf_op jit(solution)/shard_map/ppermute | solution.py:430
  14.4 0.2 collective-permute-done.3.c
  14.6 0.1 sum_x.1.mine
  14.7 7.0 %collective-permute-start.4 = (bf16[128,512]{1,0:T(8,128)(2,1)S(1)}, bf16[128,512]{1,0:T(8,128)(2,1)S(1)}, u32[]{:S(2)}, u32[]{:S(2)}) collective-permute-start(bf16[128,512]{1,0:T(8,128)(2,1)S(1)} %sum_x.1.mine), channel_id=1, source_target_pairs={{0,8},{8,0},{1,9},{9,1},{2,10},{10,2},{3,11},{11,3},{4,12},{12,4},... | collective-permute-start | bytes 393224 | tf_op jit(solution)/shard_map/ppermute | solution.py:434
  21.7 1.5 %collective-permute-start.6 = (bf16[128,512]{1,0:T(8,128)(2,1)S(1)}, bf16[128,512]{1,0:T(8,128)(2,1)S(1)}, u32[]{:S(2)}, u32[]{:S(2)}) collective-permute-start(bf16[128,512]{1,0:T(8,128)(2,1)S(1)} %sum_x.1.mine), channel_id=1, source_target_pairs={{0,1},{1,0},{2,3},{3,2},{4,5},{5,4},{6,7},{7,6},{8,9},{9,8},{10,11... | collective-permute-start | bytes 393224 | tf_op jit(solution)/shard_map/ppermute | solution.py:434
  23.2 1.0 %collective-permute-done.4.mine = bf16[128,512]{1,0:T(8,128)(2,1)S(1)} collective-permute-done((bf16[128,512]{1,0:T(8,128)(2,1)S(1)}, bf16[128,512]{1,0:T(8,128)(2,1)S(1)}, u32[]{:S(2)}, u32[]{:S(2)}) %collective-permute-start.4) | collective-permute-done | bytes 131104 | tf_op jit(solution)/shard_map/ppermute | solution.py:434
  24.2 3.6 %collective-permute-start.5 = (bf16[128,512]{1,0:T(8,128)(2,1)S(1)}, bf16[128,512]{1,0:T(8,128)(2,1)S(1)}, u32[]{:S(2)}, u32[]{:S(2)}) collective-permute-start(bf16[128,512]{1,0:T(8,128)(2,1)S(1)} %collective-permute-done.4.mine), channel_id=1, source_target_pairs={{0,1},{1,0},{2,3},{3,2},{4,5},{5,4},{6,7},{7,6},{8,9},{9,8},{10,11... | collective-permute-start | bytes 393224 | tf_op jit(solution)/shard_map/ppermute | solution.py:434
  27.8 0.0 collective-permute-done.6.other
  27.8 0.6 outer.1.acc_ref
  28.4 0.4 outer_mine.1.acc_ref
  28.9 0.0 collective-permute-done.5.other
  28.9 0.5 outer_other.1
  29.4 1.4 %collective-permute-start.7 = (bf16[32,1792]{1,0:T(8,128)(2,1)S(1)}, bf16[32,1792]{1,0:T(8,128)(2,1)S(1)}, u32[]{:S(2)}, u32[]{:S(2)}) collective-permute-start(bf16[32,1792]{1,0:T(8,128)(2,1)S(1)} %get-tuple-element.27), channel_id=1, source_target_pairs={{0,64},{64,128},{128,192},{192,0},{1,65},{65,129},{129,193},{193,1... | collective-permute-start | bytes 344072 | tf_op jit(solution)/shard_map/ppermute | solution.py:430
  30.7 1.5 %collective-permute-start.8 = (bf16[32,1792]{1,0:T(8,128)(2,1)S(1)}, bf16[32,1792]{1,0:T(8,128)(2,1)S(1)}, u32[]{:S(2)}, u32[]{:S(2)}) collective-permute-start(bf16[32,1792]{1,0:T(8,128)(2,1)S(1)} %get-tuple-element.28), channel_id=1, source_target_pairs={{0,192},{64,0},{128,64},{192,128},{1,193},{65,1},{129,65},{193,129... | collective-permute-start | bytes 344072 | tf_op jit(solution)/shard_map/ppermute | solution.py:430
  32.3 1.6 %collective-permute-start.9 = (bf16[32,1792]{1,0:T(8,128)(2,1)S(1)}, bf16[32,1792]{1,0:T(8,128)(2,1)S(1)}, u32[]{:S(2)}, u32[]{:S(2)}) collective-permute-start(bf16[32,1792]{1,0:T(8,128)(2,1)S(1)} %get-tuple-element.29), channel_id=1, source_target_pairs={{0,128},{64,192},{128,0},{192,64},{1,129},{65,193},{129,1},{193,65... | collective-permute-start | bytes 344072 | tf_op jit(solution)/shard_map/ppermute | solution.py:430
  33.8 1.5 %collective-permute-done.7.a = bf16[32,1792]{1,0:T(8,128)(2,1)S(1)} collective-permute-done((bf16[32,1792]{1,0:T(8,128)(2,1)S(1)}, bf16[32,1792]{1,0:T(8,128)(2,1)S(1)}, u32[]{:S(2)}, u32[]{:S(2)}) %collective-permute-start.7) | collective-permute-done | bytes 114720 | tf_op jit(solution)/shard_map/ppermute | solution.py:430
  35.3 0.0 collective-permute-done.8.b
  35.3 3.7 %collective-permute-done.9.c = bf16[32,1792]{1,0:T(8,128)(2,1)S(1)} collective-permute-done((bf16[32,1792]{1,0:T(8,128)(2,1)S(1)}, bf16[32,1792]{1,0:T(8,128)(2,1)S(1)}, u32[]{:S(2)}, u32[]{:S(2)}) %collective-permute-start.9) | collective-permute-done | bytes 114720 | tf_op jit(solution)/shard_map/ppermute | solution.py:430
  39.0 0.1 sum_y.1
  39.0 2.1 %collective-permute-start.10 = (bf16[16,896]{1,0:T(8,128)(2,1)S(1)}, bf16[16,896]{1,0:T(8,128)(2,1)S(1)}, u32[]{:S(2)}, u32[]{:S(2)}) collective-permute-start(bf16[16,896]{1,0:T(8,128)(2,1)S(1)} %get-tuple-element.31), channel_id=1, source_target_pairs={{0,16},{16,32},{32,48},{48,0},{1,17},{17,33},{33,49},{49,1},{2,18}... | collective-permute-start | bytes 86024 | tf_op jit(solution)/shard_map/ppermute | solution.py:430
  41.1 0.9 %collective-permute-start.11 = (bf16[16,896]{1,0:T(8,128)(2,1)S(1)}, bf16[16,896]{1,0:T(8,128)(2,1)S(1)}, u32[]{:S(2)}, u32[]{:S(2)}) collective-permute-start(bf16[16,896]{1,0:T(8,128)(2,1)S(1)} %get-tuple-element.32), channel_id=1, source_target_pairs={{0,32},{16,48},{32,0},{48,16},{1,33},{17,49},{33,1},{49,17},{2,34}... | collective-permute-start | bytes 86024 | tf_op jit(solution)/shard_map/ppermute | solution.py:430
  42.0 2.3 %collective-permute-start.12 = (bf16[16,896]{1,0:T(8,128)(2,1)S(1)}, bf16[16,896]{1,0:T(8,128)(2,1)S(1)}, u32[]{:S(2)}, u32[]{:S(2)}) collective-permute-start(bf16[16,896]{1,0:T(8,128)(2,1)S(1)} %get-tuple-element.33), channel_id=1, source_target_pairs={{0,48},{16,0},{32,16},{48,32},{1,49},{17,1},{33,17},{49,33},{2,50}... | collective-permute-start | bytes 86024 | tf_op jit(solution)/shard_map/ppermute | solution.py:430
  44.2 0.0 collective-permute-done.10.a
  44.2 0.8 %collective-permute-done.11.b = bf16[16,896]{1,0:T(8,128)(2,1)S(1)} collective-permute-done((bf16[16,896]{1,0:T(8,128)(2,1)S(1)}, bf16[16,896]{1,0:T(8,128)(2,1)S(1)}, u32[]{:S(2)}, u32[]{:S(2)}) %collective-permute-start.11) | collective-permute-done | bytes 28704 | tf_op jit(solution)/shard_map/ppermute | solution.py:430
  45.0 0.3 collective-permute-done.12.c
  45.4 0.0 copy-start
  45.4 0.8 %collective-permute-start.14 = (bf16[16,896]{1,0:T(8,128)(2,1)S(1)}, bf16[16,896]{1,0:T(8,128)(2,1)S(1)}, u32[]{:S(2)}, u32[]{:S(2)}) collective-permute-start(bf16[16,896]{1,0:T(8,128)(2,1)S(1)} %sum_z.1.refs_0_), channel_id=1, source_target_pairs={{0,2},{2,4},{4,6},{6,0},{1,3},{3,5},{5,7},{7,1},{8,10},{10,12},{12... | collective-permute-start | bytes 86024 | tf_op jit(solution)/shard_map/ppermute | solution.py:430
  46.2 1.9 %collective-permute-start.16 = (bf16[16,896]{1,0:T(8,128)(2,1)S(1)}, bf16[16,896]{1,0:T(8,128)(2,1)S(1)}, u32[]{:S(2)}, u32[]{:S(2)}) collective-permute-start(bf16[16,896]{1,0:T(8,128)(2,1)S(1)} %sum_z.1.refs_0_), channel_id=1, source_target_pairs={{0,4},{2,6},{4,0},{6,2},{1,5},{3,7},{5,1},{7,3},{8,12},{10,14},{12... | collective-permute-start | bytes 86024 | tf_op jit(solution)/shard_map/ppermute | solution.py:430
  48.0 0.8 %collective-permute-start.18 = (bf16[16,896]{1,0:T(8,128)(2,1)S(1)}, bf16[16,896]{1,0:T(8,128)(2,1)S(1)}, u32[]{:S(2)}, u32[]{:S(2)}) collective-permute-start(bf16[16,896]{1,0:T(8,128)(2,1)S(1)} %sum_z.1.refs_0_), channel_id=1, source_target_pairs={{0,6},{2,0},{4,2},{6,4},{1,7},{3,1},{5,3},{7,5},{8,14},{10,8},{12,... | collective-permute-start | bytes 86024 | tf_op jit(solution)/shard_map/ppermute | solution.py:430
  48.8 3.1 %collective-permute-start.13 = (bf16[16,896]{1,0:T(8,128)(2,1)S(1)}, bf16[16,896]{1,0:T(8,128)(2,1)S(1)}, u32[]{:S(2)}, u32[]{:S(2)}) collective-permute-start(bf16[16,896]{1,0:T(8,128)(2,1)S(1)} %sum_z.1.refs_0_), channel_id=1, source_target_pairs={{0,1},{1,0},{2,3},{3,2},{4,5},{5,4},{6,7},{7,6},{8,9},{9,8},{10,11... | collective-permute-start | bytes 86024 | tf_op jit(solution)/shard_map/ppermute | solution.py:434
  51.9 0.0 collective-permute-done.14.refs_2_
  51.9 0.9 %collective-permute-start.15 = (bf16[16,896]{1,0:T(8,128)(2,1)S(1)}, bf16[16,896]{1,0:T(8,128)(2,1)S(1)}, u32[]{:S(2)}, u32[]{:S(2)}) collective-permute-start(bf16[16,896]{1,0:T(8,128)(2,1)S(1)} %collective-permute-done.14.refs_2_), channel_id=1, source_target_pairs={{0,1},{1,0},{2,3},{3,2},{4,5},{5,4},{6,7},{7,6},{8,9},{9,8},{10,11... | collective-permute-start | bytes 86024 | tf_op jit(solution)/shard_map/ppermute | solution.py:434
  52.8 0.0 collective-permute-done.16.refs_4_
  52.8 1.5 %collective-permute-start.17 = (bf16[16,896]{1,0:T(8,128)(2,1)S(1)}, bf16[16,896]{1,0:T(8,128)(2,1)S(1)}, u32[]{:S(2)}, u32[]{:S(2)}) collective-permute-start(bf16[16,896]{1,0:T(8,128)(2,1)S(1)} %collective-permute-done.16.refs_4_), channel_id=1, source_target_pairs={{0,1},{1,0},{2,3},{3,2},{4,5},{5,4},{6,7},{7,6},{8,9},{9,8},{10,11... | collective-permute-start | bytes 86024 | tf_op jit(solution)/shard_map/ppermute | solution.py:434
  54.3 0.0 collective-permute-done.18.refs_6_
  54.3 0.8 %collective-permute-start.19 = (bf16[16,896]{1,0:T(8,128)(2,1)S(1)}, bf16[16,896]{1,0:T(8,128)(2,1)S(1)}, u32[]{:S(2)}, u32[]{:S(2)}) collective-permute-start(bf16[16,896]{1,0:T(8,128)(2,1)S(1)} %collective-permute-done.18.refs_6_), channel_id=1, source_target_pairs={{0,1},{1,0},{2,3},{3,2},{4,5},{5,4},{6,7},{7,6},{8,9},{9,8},{10,11... | collective-permute-start | bytes 86024 | tf_op jit(solution)/shard_map/ppermute | solution.py:434
  55.1 1.1 %tables.1 = (bf16[256,256]{1,0:T(8,128)(2,1)S(1)}, bf16[512,448]{1,0:T(8,128)(2,1)S(1)}) custom-call(bf16[8,256,256]{2,1,0:T(8,128)(2,1)} %constant.6.clone.win_hbm, bf16[16,512,448]{2,1,0:T(8,128)(2,1)} %constant.7.clone.mix_hbm), custom_call_target="tpu_custom_call" | custom-call | tf_op jit(solution)/shard_map/tables/pallas_call | solution.py:355
  56.2 0.0 collective-permute-done.13.refs_1_
  56.2 0.0 collective-permute-done.15.refs_3_
  56.2 0.0 collective-permute-done.17.refs_5_
  56.3 0.0 collective-permute-done.19.refs_7_
  56.3 0.7 rotate.1
  57.0 17.4 %all_to_all.11 = f32[32,8,128]{2,1,0:T(8,128)S(1)} all-to-all(f32[32,8,128]{2,1,0:T(8,128)S(1)} %bitcast.4), channel_id=1, replica_groups=mesh['y'=4,'zl'=4,'zh'=2,'x'=4,'core'=2] {'y','zl','zh'}, dimensions={0} | all-to-all | bytes 262144 | tf_op jit(solution)/shard_map/all_to_all | solution.py:452
  74.4 0.0 copy-done
  74.4 0.8 %finish.1 = f32[112,128]{1,0:T(8,128)} custom-call(f32[256,128]{1,0:T(8,128)S(1)} %bitcast.3, bf16[128,128]{1,0:T(8,128)(2,1)S(1)} %copy-done), custom_call_target="tpu_custom_call" | custom-call | tf_op jit(solution)/shard_map/finish/pallas_call | solution.py:419
  (2 shorter events, 0.1 us)
Async XLA Ops:
  2.2 4.3 %collective-permute-start = (bf16[512,128]{1,0:T(8,128)(2,1)S(1)}, bf16[512,128]{1,0:T(8,128)(2,1)S(1)}, u32[]{:S(2)}, u32[]{:S(2)}) collective-permute-start(bf16[512,128]{1,0:T(8,128)(2,1)S(1)} %get-tuple-element.22), channel_id=1, source_target_pairs={{0,1},{1,0},{2,3},{3,2},{4,5},{5,4},{6,7},{7,6},{8,9},{9,8},{10,11... | collective-permute-start | bytes 393224 | tf_op jit(solution)/shard_map/ppermute | solution.py:434
  6.5 6.0 %collective-permute-start.1 = (bf16[512,128]{1,0:T(8,128)(2,1)S(1)}, bf16[512,128]{1,0:T(8,128)(2,1)S(1)}, u32[]{:S(2)}, u32[]{:S(2)}) collective-permute-start(bf16[512,128]{1,0:T(8,128)(2,1)S(1)} %get-tuple-element.24), channel_id=1, source_target_pairs={{0,2},{2,4},{4,6},{6,0},{1,3},{3,5},{5,7},{7,1},{8,10},{10,12},{12... | collective-permute-start | bytes 393224 | tf_op jit(solution)/shard_map/ppermute | solution.py:430
  6.6 7.8 %collective-permute-start.2 = (bf16[512,128]{1,0:T(8,128)(2,1)S(1)}, bf16[512,128]{1,0:T(8,128)(2,1)S(1)}, u32[]{:S(2)}, u32[]{:S(2)}) collective-permute-start(bf16[512,128]{1,0:T(8,128)(2,1)S(1)} %get-tuple-element.24), channel_id=1, source_target_pairs={{0,6},{2,0},{4,2},{6,4},{1,7},{3,1},{5,3},{7,5},{8,14},{10,8},{12,... | collective-permute-start | bytes 393224 | tf_op jit(solution)/shard_map/ppermute | solution.py:430
  9.3 5.3 %collective-permute-start.3 = (bf16[512,128]{1,0:T(8,128)(2,1)S(1)}, bf16[512,128]{1,0:T(8,128)(2,1)S(1)}, u32[]{:S(2)}, u32[]{:S(2)}) collective-permute-start(bf16[512,128]{1,0:T(8,128)(2,1)S(1)} %get-tuple-element.24), channel_id=1, source_target_pairs={{0,4},{2,6},{4,0},{6,2},{1,5},{3,7},{5,1},{7,3},{8,12},{10,14},{12... | collective-permute-start | bytes 393224 | tf_op jit(solution)/shard_map/ppermute | solution.py:430
  14.7 9.4 %collective-permute-start.4 = (bf16[128,512]{1,0:T(8,128)(2,1)S(1)}, bf16[128,512]{1,0:T(8,128)(2,1)S(1)}, u32[]{:S(2)}, u32[]{:S(2)}) collective-permute-start(bf16[128,512]{1,0:T(8,128)(2,1)S(1)} %sum_x.1.mine), channel_id=1, source_target_pairs={{0,8},{8,0},{1,9},{9,1},{2,10},{10,2},{3,11},{11,3},{4,12},{12,4},... | collective-permute-start | bytes 393224 | tf_op jit(solution)/shard_map/ppermute | solution.py:434
  21.7 6.1 %collective-permute-start.6 = (bf16[128,512]{1,0:T(8,128)(2,1)S(1)}, bf16[128,512]{1,0:T(8,128)(2,1)S(1)}, u32[]{:S(2)}, u32[]{:S(2)}) collective-permute-start(bf16[128,512]{1,0:T(8,128)(2,1)S(1)} %sum_x.1.mine), channel_id=1, source_target_pairs={{0,1},{1,0},{2,3},{3,2},{4,5},{5,4},{6,7},{7,6},{8,9},{9,8},{10,11... | collective-permute-start | bytes 393224 | tf_op jit(solution)/shard_map/ppermute | solution.py:434
  24.2 4.7 %collective-permute-start.5 = (bf16[128,512]{1,0:T(8,128)(2,1)S(1)}, bf16[128,512]{1,0:T(8,128)(2,1)S(1)}, u32[]{:S(2)}, u32[]{:S(2)}) collective-permute-start(bf16[128,512]{1,0:T(8,128)(2,1)S(1)} %collective-permute-done.4.mine), channel_id=1, source_target_pairs={{0,1},{1,0},{2,3},{3,2},{4,5},{5,4},{6,7},{7,6},{8,9},{9,8},{10,11... | collective-permute-start | bytes 393224 | tf_op jit(solution)/shard_map/ppermute | solution.py:434
  29.4 5.9 %collective-permute-start.7 = (bf16[32,1792]{1,0:T(8,128)(2,1)S(1)}, bf16[32,1792]{1,0:T(8,128)(2,1)S(1)}, u32[]{:S(2)}, u32[]{:S(2)}) collective-permute-start(bf16[32,1792]{1,0:T(8,128)(2,1)S(1)} %get-tuple-element.27), channel_id=1, source_target_pairs={{0,64},{64,128},{128,192},{192,0},{1,65},{65,129},{129,193},{193,1... | collective-permute-start | bytes 344072 | tf_op jit(solution)/shard_map/ppermute | solution.py:430
  30.7 4.5 %collective-permute-start.8 = (bf16[32,1792]{1,0:T(8,128)(2,1)S(1)}, bf16[32,1792]{1,0:T(8,128)(2,1)S(1)}, u32[]{:S(2)}, u32[]{:S(2)}) collective-permute-start(bf16[32,1792]{1,0:T(8,128)(2,1)S(1)} %get-tuple-element.28), channel_id=1, source_target_pairs={{0,192},{64,0},{128,64},{192,128},{1,193},{65,1},{129,65},{193,129... | collective-permute-start | bytes 344072 | tf_op jit(solution)/shard_map/ppermute | solution.py:430
  32.3 6.7 %collective-permute-start.9 = (bf16[32,1792]{1,0:T(8,128)(2,1)S(1)}, bf16[32,1792]{1,0:T(8,128)(2,1)S(1)}, u32[]{:S(2)}, u32[]{:S(2)}) collective-permute-start(bf16[32,1792]{1,0:T(8,128)(2,1)S(1)} %get-tuple-element.29), channel_id=1, source_target_pairs={{0,128},{64,192},{128,0},{192,64},{1,129},{65,193},{129,1},{193,65... | collective-permute-start | bytes 344072 | tf_op jit(solution)/shard_map/ppermute | solution.py:430
  39.0 5.2 %collective-permute-start.10 = (bf16[16,896]{1,0:T(8,128)(2,1)S(1)}, bf16[16,896]{1,0:T(8,128)(2,1)S(1)}, u32[]{:S(2)}, u32[]{:S(2)}) collective-permute-start(bf16[16,896]{1,0:T(8,128)(2,1)S(1)} %get-tuple-element.31), channel_id=1, source_target_pairs={{0,16},{16,32},{32,48},{48,0},{1,17},{17,33},{33,49},{49,1},{2,18}... | collective-permute-start | bytes 86024 | tf_op jit(solution)/shard_map/ppermute | solution.py:430
  41.1 3.9 %collective-permute-start.11 = (bf16[16,896]{1,0:T(8,128)(2,1)S(1)}, bf16[16,896]{1,0:T(8,128)(2,1)S(1)}, u32[]{:S(2)}, u32[]{:S(2)}) collective-permute-start(bf16[16,896]{1,0:T(8,128)(2,1)S(1)} %get-tuple-element.32), channel_id=1, source_target_pairs={{0,32},{16,48},{32,0},{48,16},{1,33},{17,49},{33,1},{49,17},{2,34}... | collective-permute-start | bytes 86024 | tf_op jit(solution)/shard_map/ppermute | solution.py:430
  42.0 3.4 %collective-permute-start.12 = (bf16[16,896]{1,0:T(8,128)(2,1)S(1)}, bf16[16,896]{1,0:T(8,128)(2,1)S(1)}, u32[]{:S(2)}, u32[]{:S(2)}) collective-permute-start(bf16[16,896]{1,0:T(8,128)(2,1)S(1)} %get-tuple-element.33), channel_id=1, source_target_pairs={{0,48},{16,0},{32,16},{48,32},{1,49},{17,1},{33,17},{49,33},{2,50}... | collective-permute-start | bytes 86024 | tf_op jit(solution)/shard_map/ppermute | solution.py:430
  45.4 29.0 %copy-start = (bf16[128,128]{1,0:T(8,128)(2,1)S(1)}, bf16[128,128]{1,0:T(8,128)(2,1)}, u32[]{:S(2)}) copy-start(bf16[128,128]{1,0:T(8,128)(2,1)} %constant.8.clone.h_ref) | copy-start | bytes 98308
  45.4 6.5 %collective-permute-start.14 = (bf16[16,896]{1,0:T(8,128)(2,1)S(1)}, bf16[16,896]{1,0:T(8,128)(2,1)S(1)}, u32[]{:S(2)}, u32[]{:S(2)}) collective-permute-start(bf16[16,896]{1,0:T(8,128)(2,1)S(1)} %sum_z.1.refs_0_), channel_id=1, source_target_pairs={{0,2},{2,4},{4,6},{6,0},{1,3},{3,5},{5,7},{7,1},{8,10},{10,12},{12... | collective-permute-start | bytes 86024 | tf_op jit(solution)/shard_map/ppermute | solution.py:430
  46.2 6.6 %collective-permute-start.16 = (bf16[16,896]{1,0:T(8,128)(2,1)S(1)}, bf16[16,896]{1,0:T(8,128)(2,1)S(1)}, u32[]{:S(2)}, u32[]{:S(2)}) collective-permute-start(bf16[16,896]{1,0:T(8,128)(2,1)S(1)} %sum_z.1.refs_0_), channel_id=1, source_target_pairs={{0,4},{2,6},{4,0},{6,2},{1,5},{3,7},{5,1},{7,3},{8,12},{10,14},{12... | collective-permute-start | bytes 86024 | tf_op jit(solution)/shard_map/ppermute | solution.py:430
  48.0 6.3 %collective-permute-start.18 = (bf16[16,896]{1,0:T(8,128)(2,1)S(1)}, bf16[16,896]{1,0:T(8,128)(2,1)S(1)}, u32[]{:S(2)}, u32[]{:S(2)}) collective-permute-start(bf16[16,896]{1,0:T(8,128)(2,1)S(1)} %sum_z.1.refs_0_), channel_id=1, source_target_pairs={{0,6},{2,0},{4,2},{6,4},{1,7},{3,1},{5,3},{7,5},{8,14},{10,8},{12,... | collective-permute-start | bytes 86024 | tf_op jit(solution)/shard_map/ppermute | solution.py:430
  48.8 7.4 %collective-permute-start.13 = (bf16[16,896]{1,0:T(8,128)(2,1)S(1)}, bf16[16,896]{1,0:T(8,128)(2,1)S(1)}, u32[]{:S(2)}, u32[]{:S(2)}) collective-permute-start(bf16[16,896]{1,0:T(8,128)(2,1)S(1)} %sum_z.1.refs_0_), channel_id=1, source_target_pairs={{0,1},{1,0},{2,3},{3,2},{4,5},{5,4},{6,7},{7,6},{8,9},{9,8},{10,11... | collective-permute-start | bytes 86024 | tf_op jit(solution)/shard_map/ppermute | solution.py:434
  51.9 4.4 %collective-permute-start.15 = (bf16[16,896]{1,0:T(8,128)(2,1)S(1)}, bf16[16,896]{1,0:T(8,128)(2,1)S(1)}, u32[]{:S(2)}, u32[]{:S(2)}) collective-permute-start(bf16[16,896]{1,0:T(8,128)(2,1)S(1)} %collective-permute-done.14.refs_2_), channel_id=1, source_target_pairs={{0,1},{1,0},{2,3},{3,2},{4,5},{5,4},{6,7},{7,6},{8,9},{9,8},{10,11... | collective-permute-start | bytes 86024 | tf_op jit(solution)/shard_map/ppermute | solution.py:434
  52.8 3.5 %collective-permute-start.17 = (bf16[16,896]{1,0:T(8,128)(2,1)S(1)}, bf16[16,896]{1,0:T(8,128)(2,1)S(1)}, u32[]{:S(2)}, u32[]{:S(2)}) collective-permute-start(bf16[16,896]{1,0:T(8,128)(2,1)S(1)} %collective-permute-done.16.refs_4_), channel_id=1, source_target_pairs={{0,1},{1,0},{2,3},{3,2},{4,5},{5,4},{6,7},{7,6},{8,9},{9,8},{10,11... | collective-permute-start | bytes 86024 | tf_op jit(solution)/shard_map/ppermute | solution.py:434
  54.3 2.0 %collective-permute-start.19 = (bf16[16,896]{1,0:T(8,128)(2,1)S(1)}, bf16[16,896]{1,0:T(8,128)(2,1)S(1)}, u32[]{:S(2)}, u32[]{:S(2)}) collective-permute-start(bf16[16,896]{1,0:T(8,128)(2,1)S(1)} %collective-permute-done.18.refs_6_), channel_id=1, source_target_pairs={{0,1},{1,0},{2,3},{3,2},{4,5},{5,4},{6,7},{7,6},{8,9},{9,8},{10,11... | collective-permute-start | bytes 86024 | tf_op jit(solution)/shard_map/ppermute | solution.py:434

commit v4 on v3

--- a/solution.py
+++ b/solution.py
@@ -331,6 +331,21 @@
     )(own, *terms, signs)
 
 
+def pair_kernel(a, b, out_ref):
+    out_ref[...] = jnp.concatenate([a[...], b[...]], axis=0)
+
+
+def pair_up(a, b):
+    return pl.pallas_call(
+        pair_kernel,
+        in_specs=[VMEM] * 2,
+        out_specs=VMEM,
+        out_shape=jax.ShapeDtypeStruct((4 * GROUP, FOLDED), BF),
+        compiler_params=LITTLE,
+        name="pair",
+    )(a, b)
+
+
 def split_dot(lhs, value):
     high = value.astype(BF)
     low = (value - high.astype(F32)).astype(BF)
@@ -367,9 +382,12 @@
 
 
 def rotate_kernel(*refs):
-    slots, (win_ref, mix_ref, out_ref) = refs[:N_XC], refs[N_XC:]
+    slots, (win_ref, mix_ref, out_ref) = refs[:RING], refs[RING:]
     member = lax.axis_index("x") * 2 + lax.axis_index("core")
-    g = jnp.concatenate([unpack(ref[...]) for ref in slots], axis=0).astype(BF)
+    g = jnp.concatenate(
+        [unpack(part) for ref in slots for part in (ref[: 2 * GROUP, :], ref[2 * GROUP :, :])],
+        axis=0,
+    ).astype(BF)
     window = win_ref[...]
     parts = []
     for j in range(N_Q):
@@ -393,7 +411,7 @@
 def rotate(slots, window, mix):
     return pl.pallas_call(
         rotate_kernel,
-        in_specs=[VMEM] * (N_XC + 2),
+        in_specs=[VMEM] * (RING + 2),
         out_specs=VMEM,
         out_shape=jax.ShapeDtypeStruct((2 * LANE, LANE), F32),
         compiler_params=LITTLE,
@@ -446,9 +464,8 @@
     own, *sends = sum_y(own, [shift(sends[s - 1], "y", s) for s in (1, 3, 2)])
     g = sum_z(own, [shift(x, "zl", s + 1) for s, x in enumerate(sends)], sign)
 
-    ring = [g] + [shift(g, "x", s) for s in (1, 2, 3)]
-    slots = [part for x in ring for part in (x, swap(x, "core"))]
-    turned = rotate(slots, *tables())
+    g = pair_up(g, swap(g, "core"))
+    turned = rotate([g] + [shift(g, "x", s) for s in (1, 2, 3)], *tables())
     turned = lax.all_to_all(turned, ("y", "zl", "zh"), split_axis=0, concat_axis=0, tiled=True)
     return finish(turned, jnp.asarray(sylvester(COLS), BF))
 

time: 75.4 us -> 75.4 us (level); the launches traced: 75.2 us -> 74.2 us
  starting transfers between devices: 37.5 us -> 33.8 us
  waiting for transfers between devices: 13.6 us -> 16.7 us
    ppermute x8 -> x5, starting transfers between devices: 21.6 us -> 17.7 us  [swap(): return lax.ppermute(x, axis, [(0, 1), (1, 0)])]
    ppermute x12, waiting for transfers between devices: 11.6 us -> 13.8 us  [shift(): return lax.ppermute(x, axis, [(i, (i + s) % RING) for i in range(RING)])]
    ppermute x8 -> x5, waiting for transfers between devices: 1.99 us -> 2.84 us  [swap(): return lax.ppermute(x, axis, [(0, 1), (1, 0)])]
  transfers between devices with their start and end apart: 20 -> 17, of which waited for: 9 -> 12; matrix products, arithmetic and copies ran while one was open for 0% -> 0% of each run, Pallas kernels for 3% -> 3%
where the time goes in v4:
time: 75.4 us; the launch traced here: 74.2 us
  starting transfers between devices  33.8 us (45%)
  blocking collectives  17 us (23%)
  waiting for transfers between devices  16.7 us (22%)
  Pallas kernels  6.62 us (9%)
    ppermute x5, starting transfers between devices, swap(): return lax.ppermute(x, axis, [(0, 1), (1, 0)])  17.7 us
    all_to_all x1, blocking collectives, body(): lax.all_to_all(turned, ('y', 'zl', 'zh'), split_axis=0, concat_axis=0, ti...  17 us
    ppermute x12, starting transfers between devices, shift(): return lax.ppermute(x, axis, [(i, (i + s) % RING) for i in range(RING)])  16.1 us
    ppermute x12, waiting for transfers between devices, shift(): return lax.ppermute(x, axis, [(i, (i + s) % RING) for i in range(RING)])  13.8 us
    ppermute x5, waiting for transfers between devices, swap(): return lax.ppermute(x, axis, [(0, 1), (1, 0)])  2.84 us
    pallas_call x1, Pallas kernels, fold(): pl.pallas_call(fold_kernel, in_specs=[HBM, HBM], out_specs=[VMEM] * 4, ou...  2.17 us
  transfers between devices with their start and end apart: 17, of which 12 were waited for; matrix products, arithmetic and copies ran while one was open for 0% of the time, Pallas kernels for 3%

profile of v4, /device:TPU:1, one launch (start us, length us, event | category | flops | bytes accessed | tf_op | source)
XLA Modules:
  0.0 74.2 jit_solution(4159466607750557006)
XLA Ops:
  0.0 2.2 %fold.1 = (bf16[512,128]{1,0:T(8,128)(2,1)S(1)}, f32[512,128]{1,0:T(8,128)S(1)}, bf16[1024,1792]{1,0:T(8,128)(2,1)S(1)}, f32[14,128]{1,0:T(8,128)S(1)}) custom-call(bf16[1024,1792]{1,0:T(8,128)(2,1)} %x_ref.1, s32[14,128]{1,0:T(8,128)} %bitcast.5), custom_call_target="tpu_custom_call" | custom-call | flops 3670016 | bytes 3670016 | tf_op jit(solution)/shard_map/fold/pallas_call | solution.py:143
  2.2 3.3 %collective-permute-start = (bf16[512,128]{1,0:T(8,128)(2,1)S(1)}, bf16[512,128]{1,0:T(8,128)(2,1)S(1)}, u32[]{:S(2)}, u32[]{:S(2)}) collective-permute-start(bf16[512,128]{1,0:T(8,128)(2,1)S(1)} %get-tuple-element.22), channel_id=1, source_target_pairs={{0,1},{1,0},{2,3},{3,2},{4,5},{5,4},{6,7},{7,6},{8,9},{9,8},{10,11... | collective-permute-start | bytes 393224 | tf_op jit(solution)/shard_map/ppermute | solution.py:452
  5.5 1.0 %collective-permute-done.a = bf16[512,128]{1,0:T(8,128)(2,1)S(1)} collective-permute-done((bf16[512,128]{1,0:T(8,128)(2,1)S(1)}, bf16[512,128]{1,0:T(8,128)(2,1)S(1)}, u32[]{:S(2)}, u32[]{:S(2)}) %collective-permute-start) | collective-permute-done | bytes 131104 | tf_op jit(solution)/shard_map/ppermute | solution.py:452
  6.5 0.1 collective-permute-start.1
  6.6 2.7 %collective-permute-start.2 = (bf16[512,128]{1,0:T(8,128)(2,1)S(1)}, bf16[512,128]{1,0:T(8,128)(2,1)S(1)}, u32[]{:S(2)}, u32[]{:S(2)}) collective-permute-start(bf16[512,128]{1,0:T(8,128)(2,1)S(1)} %get-tuple-element.24), channel_id=1, source_target_pairs={{0,6},{2,0},{4,2},{6,4},{1,7},{3,1},{5,3},{7,5},{8,14},{10,8},{12,... | collective-permute-start | bytes 393224 | tf_op jit(solution)/shard_map/ppermute | solution.py:448
  9.3 0.0 collective-permute-start.3
  9.3 3.3 %collective-permute-done.1.a = bf16[512,128]{1,0:T(8,128)(2,1)S(1)} collective-permute-done((bf16[512,128]{1,0:T(8,128)(2,1)S(1)}, bf16[512,128]{1,0:T(8,128)(2,1)S(1)}, u32[]{:S(2)}, u32[]{:S(2)}) %collective-permute-start.1) | collective-permute-done | bytes 131104 | tf_op jit(solution)/shard_map/ppermute | solution.py:448
  12.5 1.9 %collective-permute-done.2.b = bf16[512,128]{1,0:T(8,128)(2,1)S(1)} collective-permute-done((bf16[512,128]{1,0:T(8,128)(2,1)S(1)}, bf16[512,128]{1,0:T(8,128)(2,1)S(1)}, u32[]{:S(2)}, u32[]{:S(2)}) %collective-permute-start.2) | collective-permute-done | bytes 131104 | tf_op jit(solution)/shard_map/ppermute | solution.py:448
  14.4 0.2 collective-permute-done.3.c
  14.6 0.1 sum_x.1.mine
  14.7 7.0 %collective-permute-start.4 = (bf16[128,512]{1,0:T(8,128)(2,1)S(1)}, bf16[128,512]{1,0:T(8,128)(2,1)S(1)}, u32[]{:S(2)}, u32[]{:S(2)}) collective-permute-start(bf16[128,512]{1,0:T(8,128)(2,1)S(1)} %sum_x.1.mine), channel_id=1, source_target_pairs={{0,8},{8,0},{1,9},{9,1},{2,10},{10,2},{3,11},{11,3},{4,12},{12,4},... | collective-permute-start | bytes 393224 | tf_op jit(solution)/shard_map/ppermute | solution.py:452
  21.7 1.5 %collective-permute-start.6 = (bf16[128,512]{1,0:T(8,128)(2,1)S(1)}, bf16[128,512]{1,0:T(8,128)(2,1)S(1)}, u32[]{:S(2)}, u32[]{:S(2)}) collective-permute-start(bf16[128,512]{1,0:T(8,128)(2,1)S(1)} %sum_x.1.mine), channel_id=1, source_target_pairs={{0,1},{1,0},{2,3},{3,2},{4,5},{5,4},{6,7},{7,6},{8,9},{9,8},{10,11... | collective-permute-start | bytes 393224 | tf_op jit(solution)/shard_map/ppermute | solution.py:452
  23.2 1.0 %collective-permute-done.4.mine = bf16[128,512]{1,0:T(8,128)(2,1)S(1)} collective-permute-done((bf16[128,512]{1,0:T(8,128)(2,1)S(1)}, bf16[128,512]{1,0:T(8,128)(2,1)S(1)}, u32[]{:S(2)}, u32[]{:S(2)}) %collective-permute-start.4) | collective-permute-done | bytes 131104 | tf_op jit(solution)/shard_map/ppermute | solution.py:452
  24.2 3.6 %collective-permute-start.5 = (bf16[128,512]{1,0:T(8,128)(2,1)S(1)}, bf16[128,512]{1,0:T(8,128)(2,1)S(1)}, u32[]{:S(2)}, u32[]{:S(2)}) collective-permute-start(bf16[128,512]{1,0:T(8,128)(2,1)S(1)} %collective-permute-done.4.mine), channel_id=1, source_target_pairs={{0,1},{1,0},{2,3},{3,2},{4,5},{5,4},{6,7},{7,6},{8,9},{9,8},{10,11... | collective-permute-start | bytes 393224 | tf_op jit(solution)/shard_map/ppermute | solution.py:452
  27.8 0.0 collective-permute-done.6.other
  27.8 0.6 outer.1.acc_ref
  28.4 0.4 outer_mine.1.acc_ref
  28.9 0.0 collective-permute-done.5.other
  28.9 0.5 outer_other.1
  29.4 1.4 %collective-permute-start.7 = (bf16[32,1792]{1,0:T(8,128)(2,1)S(1)}, bf16[32,1792]{1,0:T(8,128)(2,1)S(1)}, u32[]{:S(2)}, u32[]{:S(2)}) collective-permute-start(bf16[32,1792]{1,0:T(8,128)(2,1)S(1)} %get-tuple-element.27), channel_id=1, source_target_pairs={{0,64},{64,128},{128,192},{192,0},{1,65},{65,129},{129,193},{193,1... | collective-permute-start | bytes 344072 | tf_op jit(solution)/shard_map/ppermute | solution.py:448
  30.7 1.5 %collective-permute-start.8 = (bf16[32,1792]{1,0:T(8,128)(2,1)S(1)}, bf16[32,1792]{1,0:T(8,128)(2,1)S(1)}, u32[]{:S(2)}, u32[]{:S(2)}) collective-permute-start(bf16[32,1792]{1,0:T(8,128)(2,1)S(1)} %get-tuple-element.28), channel_id=1, source_target_pairs={{0,192},{64,0},{128,64},{192,128},{1,193},{65,1},{129,65},{193,129... | collective-permute-start | bytes 344072 | tf_op jit(solution)/shard_map/ppermute | solution.py:448
  32.3 1.6 %collective-permute-start.9 = (bf16[32,1792]{1,0:T(8,128)(2,1)S(1)}, bf16[32,1792]{1,0:T(8,128)(2,1)S(1)}, u32[]{:S(2)}, u32[]{:S(2)}) collective-permute-start(bf16[32,1792]{1,0:T(8,128)(2,1)S(1)} %get-tuple-element.29), channel_id=1, source_target_pairs={{0,128},{64,192},{128,0},{192,64},{1,129},{65,193},{129,1},{193,65... | collective-permute-start | bytes 344072 | tf_op jit(solution)/shard_map/ppermute | solution.py:448
  33.8 1.5 %collective-permute-done.7.a = bf16[32,1792]{1,0:T(8,128)(2,1)S(1)} collective-permute-done((bf16[32,1792]{1,0:T(8,128)(2,1)S(1)}, bf16[32,1792]{1,0:T(8,128)(2,1)S(1)}, u32[]{:S(2)}, u32[]{:S(2)}) %collective-permute-start.7) | collective-permute-done | bytes 114720 | tf_op jit(solution)/shard_map/ppermute | solution.py:448
  35.3 0.0 collective-permute-done.8.b
  35.3 3.7 %collective-permute-done.9.c = bf16[32,1792]{1,0:T(8,128)(2,1)S(1)} collective-permute-done((bf16[32,1792]{1,0:T(8,128)(2,1)S(1)}, bf16[32,1792]{1,0:T(8,128)(2,1)S(1)}, u32[]{:S(2)}, u32[]{:S(2)}) %collective-permute-start.9) | collective-permute-done | bytes 114720 | tf_op jit(solution)/shard_map/ppermute | solution.py:448
  39.0 0.1 sum_y.1
  39.0 2.1 %collective-permute-start.10 = (bf16[16,896]{1,0:T(8,128)(2,1)S(1)}, bf16[16,896]{1,0:T(8,128)(2,1)S(1)}, u32[]{:S(2)}, u32[]{:S(2)}) collective-permute-start(bf16[16,896]{1,0:T(8,128)(2,1)S(1)} %get-tuple-element.31), channel_id=1, source_target_pairs={{0,16},{16,32},{32,48},{48,0},{1,17},{17,33},{33,49},{49,1},{2,18}... | collective-permute-start | bytes 86024 | tf_op jit(solution)/shard_map/ppermute | solution.py:448
  41.1 0.9 %collective-permute-start.11 = (bf16[16,896]{1,0:T(8,128)(2,1)S(1)}, bf16[16,896]{1,0:T(8,128)(2,1)S(1)}, u32[]{:S(2)}, u32[]{:S(2)}) collective-permute-start(bf16[16,896]{1,0:T(8,128)(2,1)S(1)} %get-tuple-element.32), channel_id=1, source_target_pairs={{0,32},{16,48},{32,0},{48,16},{1,33},{17,49},{33,1},{49,17},{2,34}... | collective-permute-start | bytes 86024 | tf_op jit(solution)/shard_map/ppermute | solution.py:448
  42.0 2.3 %collective-permute-start.12 = (bf16[16,896]{1,0:T(8,128)(2,1)S(1)}, bf16[16,896]{1,0:T(8,128)(2,1)S(1)}, u32[]{:S(2)}, u32[]{:S(2)}) collective-permute-start(bf16[16,896]{1,0:T(8,128)(2,1)S(1)} %get-tuple-element.33), channel_id=1, source_target_pairs={{0,48},{16,0},{32,16},{48,32},{1,49},{17,1},{33,17},{49,33},{2,50}... | collective-permute-start | bytes 86024 | tf_op jit(solution)/shard_map/ppermute | solution.py:448
  44.2 0.0 collective-permute-done.10.a
  44.2 0.8 %collective-permute-done.11.b = bf16[16,896]{1,0:T(8,128)(2,1)S(1)} collective-permute-done((bf16[16,896]{1,0:T(8,128)(2,1)S(1)}, bf16[16,896]{1,0:T(8,128)(2,1)S(1)}, u32[]{:S(2)}, u32[]{:S(2)}) %collective-permute-start.11) | collective-permute-done | bytes 28704 | tf_op jit(solution)/shard_map/ppermute | solution.py:448
  45.0 0.3 collective-permute-done.12.c
  45.4 2.3 %collective-permute-start.13 = (bf16[16,896]{1,0:T(8,128)(2,1)S(1)}, bf16[16,896]{1,0:T(8,128)(2,1)S(1)}, u32[]{:S(2)}, u32[]{:S(2)}) collective-permute-start(bf16[16,896]{1,0:T(8,128)(2,1)S(1)} %sum_z.1.a), channel_id=1, source_target_pairs={{0,1},{1,0},{2,3},{3,2},{4,5},{5,4},{6,7},{7,6},{8,9},{9,8},{10,11... | collective-permute-start | bytes 86024 | tf_op jit(solution)/shard_map/ppermute | solution.py:452
  47.7 0.9 %collective-permute-done.13.b = bf16[16,896]{1,0:T(8,128)(2,1)S(1)} collective-permute-done((bf16[16,896]{1,0:T(8,128)(2,1)S(1)}, bf16[16,896]{1,0:T(8,128)(2,1)S(1)}, u32[]{:S(2)}, u32[]{:S(2)}) %collective-permute-start.13) | collective-permute-done | bytes 28704 | tf_op jit(solution)/shard_map/ppermute | solution.py:452
  48.6 0.0 copy-start
  48.6 1.2 %collective-permute-start.14 = (bf16[32,896]{1,0:T(8,128)(2,1)S(1)}, bf16[32,896]{1,0:T(8,128)(2,1)S(1)}, u32[]{:S(2)}, u32[]{:S(2)}) collective-permute-start(bf16[32,896]{1,0:T(8,128)(2,1)S(1)} %pair.1.refs_0_), channel_id=1, source_target_pairs={{0,2},{2,4},{4,6},{6,0},{1,3},{3,5},{5,7},{7,1},{8,10},{10,12},{12... | collective-permute-start | bytes 172040 | tf_op jit(solution)/shard_map/ppermute | solution.py:448
  49.7 2.0 %collective-permute-start.15 = (bf16[32,896]{1,0:T(8,128)(2,1)S(1)}, bf16[32,896]{1,0:T(8,128)(2,1)S(1)}, u32[]{:S(2)}, u32[]{:S(2)}) collective-permute-start(bf16[32,896]{1,0:T(8,128)(2,1)S(1)} %pair.1.refs_0_), channel_id=1, source_target_pairs={{0,4},{2,6},{4,0},{6,2},{1,5},{3,7},{5,1},{7,3},{8,12},{10,14},{12... | collective-permute-start | bytes 172040 | tf_op jit(solution)/shard_map/ppermute | solution.py:448
  51.7 0.5 collective-permute-start.16
  52.2 1.1 %tables.1 = (bf16[256,256]{1,0:T(8,128)(2,1)S(1)}, bf16[512,448]{1,0:T(8,128)(2,1)S(1)}) custom-call(bf16[8,256,256]{2,1,0:T(8,128)(2,1)} %constant.6.clone.win_hbm, bf16[16,512,448]{2,1,0:T(8,128)(2,1)} %constant.7.clone.mix_hbm), custom_call_target="tpu_custom_call" | custom-call | tf_op jit(solution)/shard_map/tables/pallas_call | solution.py:370
  53.4 0.0 collective-permute-done.14.refs_1_
  53.4 1.4 %collective-permute-done.15.refs_2_ = bf16[32,896]{1,0:T(8,128)(2,1)S(1)} collective-permute-done((bf16[32,896]{1,0:T(8,128)(2,1)S(1)}, bf16[32,896]{1,0:T(8,128)(2,1)S(1)}, u32[]{:S(2)}, u32[]{:S(2)}) %collective-permute-start.15) | collective-permute-done | bytes 57376 | tf_op jit(solution)/shard_map/ppermute | solution.py:448
  54.8 0.9 %collective-permute-done.16.refs_3_ = bf16[32,896]{1,0:T(8,128)(2,1)S(1)} collective-permute-done((bf16[32,896]{1,0:T(8,128)(2,1)S(1)}, bf16[32,896]{1,0:T(8,128)(2,1)S(1)}, u32[]{:S(2)}, u32[]{:S(2)}) %collective-permute-start.16) | collective-permute-done | bytes 57376 | tf_op jit(solution)/shard_map/ppermute | solution.py:448
  55.6 0.7 rotate.1
  56.3 17.0 %all_to_all.11 = f32[32,8,128]{2,1,0:T(8,128)S(1)} all-to-all(f32[32,8,128]{2,1,0:T(8,128)S(1)} %bitcast.4), channel_id=1, replica_groups=mesh['y'=4,'zl'=4,'zh'=2,'x'=4,'core'=2] {'y','zl','zh'}, dimensions={0} | all-to-all | bytes 262144 | tf_op jit(solution)/shard_map/all_to_all | solution.py:469
  73.4 0.0 copy-done
  73.4 0.8 %finish.1 = f32[112,128]{1,0:T(8,128)} custom-call(f32[256,128]{1,0:T(8,128)S(1)} %bitcast.3, bf16[128,128]{1,0:T(8,128)(2,1)S(1)} %copy-done), custom_call_target="tpu_custom_call" | custom-call | tf_op jit(solution)/shard_map/finish/pallas_call | solution.py:437
  (3 shorter events, 0.1 us)
Async XLA Ops:
  2.2 4.3 %collective-permute-start = (bf16[512,128]{1,0:T(8,128)(2,1)S(1)}, bf16[512,128]{1,0:T(8,128)(2,1)S(1)}, u32[]{:S(2)}, u32[]{:S(2)}) collective-permute-start(bf16[512,128]{1,0:T(8,128)(2,1)S(1)} %get-tuple-element.22), channel_id=1, source_target_pairs={{0,1},{1,0},{2,3},{3,2},{4,5},{5,4},{6,7},{7,6},{8,9},{9,8},{10,11... | collective-permute-start | bytes 393224 | tf_op jit(solution)/shard_map/ppermute | solution.py:452
  6.5 6.0 %collective-permute-start.1 = (bf16[512,128]{1,0:T(8,128)(2,1)S(1)}, bf16[512,128]{1,0:T(8,128)(2,1)S(1)}, u32[]{:S(2)}, u32[]{:S(2)}) collective-permute-start(bf16[512,128]{1,0:T(8,128)(2,1)S(1)} %get-tuple-element.24), channel_id=1, source_target_pairs={{0,2},{2,4},{4,6},{6,0},{1,3},{3,5},{5,7},{7,1},{8,10},{10,12},{12... | collective-permute-start | bytes 393224 | tf_op jit(solution)/shard_map/ppermute | solution.py:448
  6.6 7.8 %collective-permute-start.2 = (bf16[512,128]{1,0:T(8,128)(2,1)S(1)}, bf16[512,128]{1,0:T(8,128)(2,1)S(1)}, u32[]{:S(2)}, u32[]{:S(2)}) collective-permute-start(bf16[512,128]{1,0:T(8,128)(2,1)S(1)} %get-tuple-element.24), channel_id=1, source_target_pairs={{0,6},{2,0},{4,2},{6,4},{1,7},{3,1},{5,3},{7,5},{8,14},{10,8},{12,... | collective-permute-start | bytes 393224 | tf_op jit(solution)/shard_map/ppermute | solution.py:448
  9.3 5.3 %collective-permute-start.3 = (bf16[512,128]{1,0:T(8,128)(2,1)S(1)}, bf16[512,128]{1,0:T(8,128)(2,1)S(1)}, u32[]{:S(2)}, u32[]{:S(2)}) collective-permute-start(bf16[512,128]{1,0:T(8,128)(2,1)S(1)} %get-tuple-element.24), channel_id=1, source_target_pairs={{0,4},{2,6},{4,0},{6,2},{1,5},{3,7},{5,1},{7,3},{8,12},{10,14},{12... | collective-permute-start | bytes 393224 | tf_op jit(solution)/shard_map/ppermute | solution.py:448
  14.7 9.4 %collective-permute-start.4 = (bf16[128,512]{1,0:T(8,128)(2,1)S(1)}, bf16[128,512]{1,0:T(8,128)(2,1)S(1)}, u32[]{:S(2)}, u32[]{:S(2)}) collective-permute-start(bf16[128,512]{1,0:T(8,128)(2,1)S(1)} %sum_x.1.mine), channel_id=1, source_target_pairs={{0,8},{8,0},{1,9},{9,1},{2,10},{10,2},{3,11},{11,3},{4,12},{12,4},... | collective-permute-start | bytes 393224 | tf_op jit(solution)/shard_map/ppermute | solution.py:452
  21.7 6.1 %collective-permute-start.6 = (bf16[128,512]{1,0:T(8,128)(2,1)S(1)}, bf16[128,512]{1,0:T(8,128)(2,1)S(1)}, u32[]{:S(2)}, u32[]{:S(2)}) collective-permute-start(bf16[128,512]{1,0:T(8,128)(2,1)S(1)} %sum_x.1.mine), channel_id=1, source_target_pairs={{0,1},{1,0},{2,3},{3,2},{4,5},{5,4},{6,7},{7,6},{8,9},{9,8},{10,11... | collective-permute-start | bytes 393224 | tf_op jit(solution)/shard_map/ppermute | solution.py:452
  24.2 4.7 %collective-permute-start.5 = (bf16[128,512]{1,0:T(8,128)(2,1)S(1)}, bf16[128,512]{1,0:T(8,128)(2,1)S(1)}, u32[]{:S(2)}, u32[]{:S(2)}) collective-permute-start(bf16[128,512]{1,0:T(8,128)(2,1)S(1)} %collective-permute-done.4.mine), channel_id=1, source_target_pairs={{0,1},{1,0},{2,3},{3,2},{4,5},{5,4},{6,7},{7,6},{8,9},{9,8},{10,11... | collective-permute-start | bytes 393224 | tf_op jit(solution)/shard_map/ppermute | solution.py:452
  29.4 5.9 %collective-permute-start.7 = (bf16[32,1792]{1,0:T(8,128)(2,1)S(1)}, bf16[32,1792]{1,0:T(8,128)(2,1)S(1)}, u32[]{:S(2)}, u32[]{:S(2)}) collective-permute-start(bf16[32,1792]{1,0:T(8,128)(2,1)S(1)} %get-tuple-element.27), channel_id=1, source_target_pairs={{0,64},{64,128},{128,192},{192,0},{1,65},{65,129},{129,193},{193,1... | collective-permute-start | bytes 344072 | tf_op jit(solution)/shard_map/ppermute | solution.py:448
  30.7 4.5 %collective-permute-start.8 = (bf16[32,1792]{1,0:T(8,128)(2,1)S(1)}, bf16[32,1792]{1,0:T(8,128)(2,1)S(1)}, u32[]{:S(2)}, u32[]{:S(2)}) collective-permute-start(bf16[32,1792]{1,0:T(8,128)(2,1)S(1)} %get-tuple-element.28), channel_id=1, source_target_pairs={{0,192},{64,0},{128,64},{192,128},{1,193},{65,1},{129,65},{193,129... | collective-permute-start | bytes 344072 | tf_op jit(solution)/shard_map/ppermute | solution.py:448
  32.3 6.7 %collective-permute-start.9 = (bf16[32,1792]{1,0:T(8,128)(2,1)S(1)}, bf16[32,1792]{1,0:T(8,128)(2,1)S(1)}, u32[]{:S(2)}, u32[]{:S(2)}) collective-permute-start(bf16[32,1792]{1,0:T(8,128)(2,1)S(1)} %get-tuple-element.29), channel_id=1, source_target_pairs={{0,128},{64,192},{128,0},{192,64},{1,129},{65,193},{129,1},{193,65... | collective-permute-start | bytes 344072 | tf_op jit(solution)/shard_map/ppermute | solution.py:448
  39.0 5.2 %collective-permute-start.10 = (bf16[16,896]{1,0:T(8,128)(2,1)S(1)}, bf16[16,896]{1,0:T(8,128)(2,1)S(1)}, u32[]{:S(2)}, u32[]{:S(2)}) collective-permute-start(bf16[16,896]{1,0:T(8,128)(2,1)S(1)} %get-tuple-element.31), channel_id=1, source_target_pairs={{0,16},{16,32},{32,48},{48,0},{1,17},{17,33},{33,49},{49,1},{2,18}... | collective-permute-start | bytes 86024 | tf_op jit(solution)/shard_map/ppermute | solution.py:448
  41.1 3.9 %collective-permute-start.11 = (bf16[16,896]{1,0:T(8,128)(2,1)S(1)}, bf16[16,896]{1,0:T(8,128)(2,1)S(1)}, u32[]{:S(2)}, u32[]{:S(2)}) collective-permute-start(bf16[16,896]{1,0:T(8,128)(2,1)S(1)} %get-tuple-element.32), channel_id=1, source_target_pairs={{0,32},{16,48},{32,0},{48,16},{1,33},{17,49},{33,1},{49,17},{2,34}... | collective-permute-start | bytes 86024 | tf_op jit(solution)/shard_map/ppermute | solution.py:448
  42.0 3.4 %collective-permute-start.12 = (bf16[16,896]{1,0:T(8,128)(2,1)S(1)}, bf16[16,896]{1,0:T(8,128)(2,1)S(1)}, u32[]{:S(2)}, u32[]{:S(2)}) collective-permute-start(bf16[16,896]{1,0:T(8,128)(2,1)S(1)} %get-tuple-element.33), channel_id=1, source_target_pairs={{0,48},{16,0},{32,16},{48,32},{1,49},{17,1},{33,17},{49,33},{2,50}... | collective-permute-start | bytes 86024 | tf_op jit(solution)/shard_map/ppermute | solution.py:448
  45.4 3.2 %collective-permute-start.13 = (bf16[16,896]{1,0:T(8,128)(2,1)S(1)}, bf16[16,896]{1,0:T(8,128)(2,1)S(1)}, u32[]{:S(2)}, u32[]{:S(2)}) collective-permute-start(bf16[16,896]{1,0:T(8,128)(2,1)S(1)} %sum_z.1.a), channel_id=1, source_target_pairs={{0,1},{1,0},{2,3},{3,2},{4,5},{5,4},{6,7},{7,6},{8,9},{9,8},{10,11... | collective-permute-start | bytes 86024 | tf_op jit(solution)/shard_map/ppermute | solution.py:452
  48.6 24.8 %copy-start = (bf16[128,128]{1,0:T(8,128)(2,1)S(1)}, bf16[128,128]{1,0:T(8,128)(2,1)}, u32[]{:S(2)}) copy-start(bf16[128,128]{1,0:T(8,128)(2,1)} %constant.8.clone.h_ref) | copy-start | bytes 98308
  48.6 4.8 %collective-permute-start.14 = (bf16[32,896]{1,0:T(8,128)(2,1)S(1)}, bf16[32,896]{1,0:T(8,128)(2,1)S(1)}, u32[]{:S(2)}, u32[]{:S(2)}) collective-permute-start(bf16[32,896]{1,0:T(8,128)(2,1)S(1)} %pair.1.refs_0_), channel_id=1, source_target_pairs={{0,2},{2,4},{4,6},{6,0},{1,3},{3,5},{5,7},{7,1},{8,10},{10,12},{12... | collective-permute-start | bytes 172040 | tf_op jit(solution)/shard_map/ppermute | solution.py:448
  49.7 5.0 %collective-permute-start.15 = (bf16[32,896]{1,0:T(8,128)(2,1)S(1)}, bf16[32,896]{1,0:T(8,128)(2,1)S(1)}, u32[]{:S(2)}, u32[]{:S(2)}) collective-permute-start(bf16[32,896]{1,0:T(8,128)(2,1)S(1)} %pair.1.refs_0_), channel_id=1, source_target_pairs={{0,4},{2,6},{4,0},{6,2},{1,5},{3,7},{5,1},{7,3},{8,12},{10,14},{12... | collective-permute-start | bytes 172040 | tf_op jit(solution)/shard_map/ppermute | solution.py:448
  51.7 3.9 %collective-permute-start.16 = (bf16[32,896]{1,0:T(8,128)(2,1)S(1)}, bf16[32,896]{1,0:T(8,128)(2,1)S(1)}, u32[]{:S(2)}, u32[]{:S(2)}) collective-permute-start(bf16[32,896]{1,0:T(8,128)(2,1)S(1)} %pair.1.refs_0_), channel_id=1, source_target_pairs={{0,6},{2,0},{4,2},{6,4},{1,7},{3,1},{5,3},{7,5},{8,14},{10,8},{12,... | collective-permute-start | bytes 172040 | tf_op jit(solution)/shard_map/ppermute | solution.py:448
